TPU v7x, 256 devices: a whole 4x4x8 slice. The times are simulated.
256 devices in a mesh: section: 4 (over y), dp: 64 (over x, z, core).
Axes of the slice: x: 4, y: 4, z: 8, core: 2. Of those that a mesh axis runs over, the one named last changes fastest.
Arguments:
- inputs: bfloat16 [4, 2048, 2048], P(None, 'dp'), may hold values from -6 to 6
- route: int32 [4, 4, 2048, 6], P('section', None, 'dp'), may hold values from 0 to 63, as said below
- gain: bfloat16 [4, 2048], P('section'), may hold values from 0.099609375 to 1.8984375
- router: bfloat16 [4, 2048, 64], P('section'), may hold values from -0.125 to 0.125
- w_gate: bfloat16 [4, 64, 2048, 768], P('section', 'dp'), may hold values from -0.125 to 0.125
- w_up: bfloat16 [4, 64, 2048, 768], P('section', 'dp'), may hold values from -0.125 to 0.125
- w_down: bfloat16 [4, 64, 768, 2048], P('section', 'dp'), may hold values from -0.21875 to 0.21875
Outputs:
- states: bfloat16 [4, 4, 2048, 2048], P('section', None, 'dp')
Inputs may be any that keep to these rules, and one draw needn't show every extreme that they name: `route`: each token names 6 different experts. Among the 32 tokens of one index of dp in one micro-batch and layer, no expert is named more than 6 times; in every micro-batch and layer one expert is named exactly 6 times by the tokens of every index of dp.
All inputs are finite; a program needn't handle non-finite values.
Results may differ from a plain program's by a relative error of at most 0.015.
Values may be sent and summed in bfloat16 or wider, within the bound.
No kernel may reach another device: no remote copies, remote signals or barrier semaphores. Data moves between devices by JAX's collectives and lax.ppermute only.
A program may use at most 128 MiB of HBM per device.

v0:
```python
import jax
import jax.numpy as jnp
from jax import lax
from jax.sharding import PartitionSpec as P

EPS = 1e-06


def shifted(x, axis, by):
    devices = lax.axis_size(axis)
    pairs = [(i, i + by) for i in range(devices) if 0 <= i + by < devices]
    return lax.ppermute(x, axis, pairs)


def expert_rows(rows, gate_mat, up_mat, down_mat):
    gate_act = jnp.dot(rows, gate_mat, preferred_element_type=jnp.float32)
    up_act = jnp.dot(rows, up_mat, preferred_element_type=jnp.float32)
    hidden = (jax.nn.silu(gate_act) * up_act).astype(jnp.bfloat16)
    return jnp.dot(hidden, down_mat, preferred_element_type=jnp.float32).astype(jnp.bfloat16)


def on_device(inputs, route, gain, router, w_gate, w_up, w_down):
    section_count = lax.axis_size("section")
    section_index = lax.axis_index("section")
    micro_count, tok_rows, model_width = inputs.shape
    top_count = route.shape[-1]
    experts = router.shape[-1]
    pair_load = 2 * tok_rows * top_count // experts
    capacity = min(pair_load, tok_rows)
    slot_count = experts * capacity
    gate_mat = w_gate[0, 0]
    up_mat = w_up[0, 0]
    down_mat = w_down[0, 0]
    gain_row = gain[0].astype(jnp.float32)
    router_mat = router[0]
    expert_ids = jnp.arange(experts, dtype=jnp.int32)
    slot_ids = jnp.arange(slot_count, dtype=jnp.int32)

    def compute_all(flat_rows):
        return expert_rows(flat_rows, gate_mat, up_mat, down_mat)

    def skip_all(flat_rows):
        return jnp.zeros_like(flat_rows)

    inbound = jnp.zeros((tok_rows, model_width), jnp.bfloat16)
    states = jnp.zeros((micro_count, tok_rows, model_width), jnp.bfloat16)
    for tick_no in range(micro_count + section_count - 1):
        micro_now = tick_no - section_index
        active = (micro_now >= 0) & (micro_now < micro_count)
        micro_index = jnp.clip(micro_now, 0, micro_count - 1)
        fresh_rows = lax.dynamic_index_in_dim(inputs, micro_index, 0, keepdims=False)
        current = jnp.where(section_index == 0, fresh_rows, inbound)
        chosen_ids = lax.dynamic_index_in_dim(route[0], micro_index, 0, keepdims=False)
        wide_state = current.astype(jnp.float32)
        inv_rms = lax.rsqrt(jnp.mean(wide_state * wide_state, axis=1, keepdims=True) + EPS)
        normed = (wide_state * inv_rms * gain_row).astype(jnp.bfloat16)
        logits = jnp.dot(normed, router_mat, preferred_element_type=jnp.float32)
        scores = jax.nn.sigmoid(jnp.take_along_axis(logits, chosen_ids, axis=1))
        weights = scores / jnp.sum(scores, axis=1, keepdims=True)
        flat_ids = chosen_ids.reshape(-1)
        onehot = (flat_ids[:, None] == expert_ids[None, :]).astype(jnp.int32)
        slot_rank = jnp.sum((jnp.cumsum(onehot, axis=0) - onehot) * onehot, axis=1)
        target = flat_ids * capacity + slot_rank
        selector = (target[None, :] == slot_ids[:, None]) & active
        by_token = jnp.sum(
            selector.reshape(slot_count, tok_rows, top_count).astype(jnp.int32), axis=2
        )
        buffer = jnp.dot(
            by_token.astype(jnp.bfloat16), normed, preferred_element_type=jnp.float32
        ).astype(jnp.bfloat16)
        live_slots = jnp.sum(by_token, axis=1).reshape(experts, capacity)
        slot_buffer = buffer.reshape(experts, capacity, model_width)
        slot_rows = lax.all_to_all(slot_buffer, "dp", split_axis=0, concat_axis=0, tiled=True)
        slot_live = lax.all_to_all(live_slots, "dp", split_axis=0, concat_axis=0, tiled=True)
        source_count, item_count = slot_live.shape
        row_count = source_count * item_count
        run_flat_rows = slot_rows.reshape(row_count, model_width)
        live_flat = slot_live.reshape(row_count)
        expert_out = lax.cond(jnp.any(live_flat > 0), compute_all, skip_all, run_flat_rows)
        expert_out = expert_out.reshape(source_count, item_count, model_width)
        returned = lax.all_to_all(expert_out, "dp", split_axis=0, concat_axis=0, tiled=True)
        copies = returned.reshape(slot_count, model_width)[target].reshape(
            tok_rows, top_count, model_width
        )
        mixed = jnp.einsum("tk,tkd->td", weights, copies.astype(jnp.float32))
        layer_out = (wide_state + mixed).astype(jnp.bfloat16)
        previous = lax.dynamic_index_in_dim(states, micro_index, 0, keepdims=False)
        states = lax.dynamic_update_index_in_dim(
            states, jnp.where(active, layer_out, previous), micro_index, 0
        )
        inbound = shifted(layer_out, "section", 1)
    return states[None]


def solution(mesh):
    in_specs = (
        P(None, "dp", None),
        P("section", None, "dp", None),
        P("section", None),
        P("section", None, None),
        P("section", "dp", None, None),
        P("section", "dp", None, None),
        P("section", "dp", None, None),
    )
    out_specs = P("section", None, "dp", None)
    return jax.shard_map(
        on_device, mesh=mesh, in_specs=in_specs, out_specs=out_specs, check_vma=False
    )
```

profile of v0, /device:TPU:1, one launch (start us, length us, event | category | flops | bytes accessed | tf_op | source)
XLA Modules:
  0.0 1047.8 jit_solution(9166134273486749376)
XLA Ops:
  5.9 13.0 %all-to-all-start = ((s32[64,1,6]{2,1,0:T(1,128)}), s32[64,1,6]{2,1,0:T(1,128)S(1)}, u32[]{:S(2)}, u32[]{:S(2)}) async-start(s32[64,1,6]{2,1,0:T(1,128)} %bitcast.8), calls=%async_computation | async-start | bytes 65536 | tf_op jit(solution)/shard_map/all_to_all | solution.py:74
  34.3 50.0 %all-to-all-done.1 = bf16[64,6,2048]{2,1,0:T(8,128)(2,1)S(1)} async-done(((bf16[64,6,2048]{2,1,0:T(8,128)(2,1)}), bf16[64,6,2048]{2,1,0:T(8,128)(2,1)S(1)}, u32[]{:S(2)}, u32[]{:S(2)}) %all-to-all-start.1) | async-done | bytes 1572896 | tf_op jit(solution)/shard_map/all_to_all | solution.py:73
  84.3 12.9 %conditional.7 = (bf16[384,2048]{1,0:T(8,128)(2,1)S(1)}) conditional(s32[]{:T(128)} %convert_element_type.244, () %tuple.48, (bf16[64,6,2048]{2,1,0:T(8,128)(2,1)S(1)}, bf16[2048,768]{1,0:T(8,128)(2,1)}, bf16[2048,768]{1,0:T(8,128)(2,1)}, bf16[768,2048]{1,0:T(8,128)(2,1)}) %tuple.124), branch_computations={%region_8.10_spmd, %region_9.11_spmd} | conditional | flops 3626434560 | bytes 19660808 | solution.py:79
  90.5 6.7 convolution_convert_fusion
  107.5 48.5 %all-to-all-done.2 = bf16[64,6,2048]{2,1,0:T(8,128)(2,1)} async-done(((bf16[64,6,2048]{2,1,0:T(8,128)(2,1)}), bf16[64,6,2048]{2,1,0:T(8,128)(2,1)}, u32[]{:S(2)}, u32[]{:S(2)}) %all-to-all-start.2) | async-done | bytes 1572896 | tf_op jit(solution)/shard_map/all_to_all | solution.py:81
  171.5 6.8 all-to-all-done.3
  189.8 45.2 %all-to-all-done.4 = bf16[64,6,2048]{2,1,0:T(8,128)(2,1)S(1)} async-done(((bf16[64,6,2048]{2,1,0:T(8,128)(2,1)}), bf16[64,6,2048]{2,1,0:T(8,128)(2,1)S(1)}, u32[]{:S(2)}, u32[]{:S(2)}) %all-to-all-start.4) | async-done | bytes 1572896 | tf_op jit(solution)/shard_map/all_to_all | solution.py:73
  235.1 12.9 %conditional.8 = (bf16[384,2048]{1,0:T(8,128)(2,1)S(1)}) conditional(s32[]{:T(128)} %convert_element_type.253, () %tuple.50, (bf16[64,6,2048]{2,1,0:T(8,128)(2,1)S(1)}, bf16[2048,768]{1,0:T(8,128)(2,1)}, bf16[2048,768]{1,0:T(8,128)(2,1)}, bf16[768,2048]{1,0:T(8,128)(2,1)}) %tuple.125), branch_computations={%region_18.20_spmd, %region_19.21_spmd} | conditional | flops 3626434560 | bytes 19660808 | solution.py:79
  241.3 6.7 convolution_convert_fusion.1
  262.3 44.5 %all-to-all-done.5 = bf16[64,6,2048]{2,1,0:T(8,128)(2,1)} async-done(((bf16[64,6,2048]{2,1,0:T(8,128)(2,1)}), bf16[64,6,2048]{2,1,0:T(8,128)(2,1)}, u32[]{:S(2)}, u32[]{:S(2)}) %all-to-all-start.5) | async-done | bytes 1572896 | tf_op jit(solution)/shard_map/all_to_all | solution.py:81
  324.5 6.8 all-to-all-done.6
  338.8 49.3 %all-to-all-done.7 = bf16[64,6,2048]{2,1,0:T(8,128)(2,1)S(1)} async-done(((bf16[64,6,2048]{2,1,0:T(8,128)(2,1)}), bf16[64,6,2048]{2,1,0:T(8,128)(2,1)S(1)}, u32[]{:S(2)}, u32[]{:S(2)}) %all-to-all-start.7) | async-done | bytes 1572896 | tf_op jit(solution)/shard_map/all_to_all | solution.py:73
  388.1 12.9 %conditional.9 = (bf16[384,2048]{1,0:T(8,128)(2,1)S(1)}) conditional(s32[]{:T(128)} %convert_element_type.261, () %tuple.52, (bf16[64,6,2048]{2,1,0:T(8,128)(2,1)S(1)}, bf16[2048,768]{1,0:T(8,128)(2,1)}, bf16[2048,768]{1,0:T(8,128)(2,1)}, bf16[768,2048]{1,0:T(8,128)(2,1)}) %tuple.126), branch_computations={%region_28.30_spmd, %region_29.31_spmd} | conditional | flops 3626434560 | bytes 19660808 | solution.py:79
  394.2 6.7 convolution_convert_fusion.2
  411.2 48.6 %all-to-all-done.8 = bf16[64,6,2048]{2,1,0:T(8,128)(2,1)} async-done(((bf16[64,6,2048]{2,1,0:T(8,128)(2,1)}), bf16[64,6,2048]{2,1,0:T(8,128)(2,1)}, u32[]{:S(2)}, u32[]{:S(2)}) %all-to-all-start.8) | async-done | bytes 1572896 | tf_op jit(solution)/shard_map/all_to_all | solution.py:81
  468.6 6.1 all-to-all-start.9
  477.2 6.7 all-to-all-done.9
  495.2 45.4 %all-to-all-done.10 = bf16[64,6,2048]{2,1,0:T(8,128)(2,1)S(1)} async-done(((bf16[64,6,2048]{2,1,0:T(8,128)(2,1)}), bf16[64,6,2048]{2,1,0:T(8,128)(2,1)S(1)}, u32[]{:S(2)}, u32[]{:S(2)}) %all-to-all-start.10) | async-done | bytes 1572896 | tf_op jit(solution)/shard_map/all_to_all | solution.py:73
  540.6 12.9 %conditional.10 = (bf16[384,2048]{1,0:T(8,128)(2,1)S(1)}) conditional(s32[]{:T(128)} %convert_element_type.269, () %tuple.54, (bf16[64,6,2048]{2,1,0:T(8,128)(2,1)S(1)}, bf16[2048,768]{1,0:T(8,128)(2,1)}, bf16[2048,768]{1,0:T(8,128)(2,1)}, bf16[768,2048]{1,0:T(8,128)(2,1)}) %tuple.127), branch_computations={%region_38.40_spmd, %region_39.41_spmd} | conditional | flops 3626434560 | bytes 19660808 | solution.py:79
  546.8 6.7 convolution_convert_fusion.3
  567.9 44.4 %all-to-all-done.11 = bf16[64,6,2048]{2,1,0:T(8,128)(2,1)} async-done(((bf16[64,6,2048]{2,1,0:T(8,128)(2,1)}), bf16[64,6,2048]{2,1,0:T(8,128)(2,1)}, u32[]{:S(2)}, u32[]{:S(2)}) %all-to-all-start.11) | async-done | bytes 1572896 | tf_op jit(solution)/shard_map/all_to_all | solution.py:81
  621.6 6.3 all-to-all-start.12
  630.4 6.7 all-to-all-done.12
  644.6 49.3 %all-to-all-done.13 = bf16[64,6,2048]{2,1,0:T(8,128)(2,1)S(1)} async-done(((bf16[64,6,2048]{2,1,0:T(8,128)(2,1)}), bf16[64,6,2048]{2,1,0:T(8,128)(2,1)S(1)}, u32[]{:S(2)}, u32[]{:S(2)}) %all-to-all-start.13) | async-done | bytes 1572896 | tf_op jit(solution)/shard_map/all_to_all | solution.py:73
  704.3 48.6 %all-to-all-done.14 = bf16[64,6,2048]{2,1,0:T(8,128)(2,1)} async-done(((bf16[64,6,2048]{2,1,0:T(8,128)(2,1)}), bf16[64,6,2048]{2,1,0:T(8,128)(2,1)}, u32[]{:S(2)}, u32[]{:S(2)}) %all-to-all-start.14) | async-done | bytes 1572896 | tf_op jit(solution)/shard_map/all_to_all | solution.py:81
  759.5 8.3 collective-permute-start.4
  777.2 6.8 all-to-all-done.15
  791.7 49.3 %all-to-all-done.16 = bf16[64,6,2048]{2,1,0:T(8,128)(2,1)S(1)} async-done(((bf16[64,6,2048]{2,1,0:T(8,128)(2,1)}), bf16[64,6,2048]{2,1,0:T(8,128)(2,1)S(1)}, u32[]{:S(2)}, u32[]{:S(2)}) %all-to-all-start.16) | async-done | bytes 1572896 | tf_op jit(solution)/shard_map/all_to_all | solution.py:73
  854.3 45.7 %all-to-all-done.17 = bf16[64,6,2048]{2,1,0:T(8,128)(2,1)} async-done(((bf16[64,6,2048]{2,1,0:T(8,128)(2,1)}), bf16[64,6,2048]{2,1,0:T(8,128)(2,1)}, u32[]{:S(2)}, u32[]{:S(2)}) %all-to-all-start.17) | async-done | bytes 1572896 | tf_op jit(solution)/shard_map/all_to_all | solution.py:81
  917.6 6.8 all-to-all-done.18
  932.1 49.3 %all-to-all-done.19 = bf16[64,6,2048]{2,1,0:T(8,128)(2,1)S(1)} async-done(((bf16[64,6,2048]{2,1,0:T(8,128)(2,1)}), bf16[64,6,2048]{2,1,0:T(8,128)(2,1)S(1)}, u32[]{:S(2)}, u32[]{:S(2)}) %all-to-all-start.19) | async-done | bytes 1572896 | tf_op jit(solution)/shard_map/all_to_all | solution.py:73
  992.5 47.9 %all-to-all-done.20 = bf16[64,6,2048]{2,1,0:T(8,128)(2,1)} async-done(((bf16[64,6,2048]{2,1,0:T(8,128)(2,1)}), bf16[64,6,2048]{2,1,0:T(8,128)(2,1)}, u32[]{:S(2)}, u32[]{:S(2)}) %all-to-all-start.20) | async-done | bytes 1572896 | tf_op jit(solution)/shard_map/all_to_all | solution.py:81
  (423 shorter events, 275.2 us)
Async XLA Ops:
  0.0 105.2 %copy-start = (bf16[1,2048,64]{1,2,0:T(8,128)(2,1)S(1)}, bf16[1,2048,64]{1,2,0:T(8,128)(2,1)}, u32[]{:S(2)}) copy-start(bf16[1,2048,64]{1,2,0:T(8,128)(2,1)} %param.26) | copy-start | bytes 786436
  0.0 20.0 %copy-start.1 = (bf16[4,32,2048]{2,1,0:T(8,128)(2,1)S(1)}, bf16[4,32,2048]{2,1,0:T(8,128)(2,1)}, u32[]{:S(2)}) copy-start(bf16[4,32,2048]{2,1,0:T(8,128)(2,1)} %param.23) | copy-start | bytes 1572868
  0.0 20.0 %copy-start.32 = (bf16[1,2048]{1,0:T(2,128)(2,1)S(1)}, bf16[1,2048]{1,0:T(2,128)(2,1)}, u32[]{:S(2)}) copy-start(bf16[1,2048]{1,0:T(2,128)(2,1)} %param.25) | copy-start | bytes 12292
  5.9 22.2 %all-to-all-start = ((s32[64,1,6]{2,1,0:T(1,128)}), s32[64,1,6]{2,1,0:T(1,128)S(1)}, u32[]{:S(2)}, u32[]{:S(2)}) async-start(s32[64,1,6]{2,1,0:T(1,128)} %bitcast.8), calls=%async_computation | async-start | bytes 65536 | tf_op jit(solution)/shard_map/all_to_all | solution.py:74
  28.1 56.2 %all-to-all-start.1 = ((bf16[64,6,2048]{2,1,0:T(8,128)(2,1)}), bf16[64,6,2048]{2,1,0:T(8,128)(2,1)S(1)}, u32[]{:S(2)}, u32[]{:S(2)}) async-start(bf16[64,6,2048]{2,1,0:T(8,128)(2,1)} %reshape.698), calls=%async_computation.1 | async-start | bytes 4194304 | tf_op jit(solution)/shard_map/all_to_all | solution.py:73
  98.8 57.2 %all-to-all-start.2 = ((bf16[64,6,2048]{2,1,0:T(8,128)(2,1)}), bf16[64,6,2048]{2,1,0:T(8,128)(2,1)}, u32[]{:S(2)}, u32[]{:S(2)}) async-start(bf16[64,6,2048]{2,1,0:T(8,128)(2,1)} %reshape.699), calls=%async_computation.2 | async-start | bytes 4194304 | tf_op jit(solution)/shard_map/all_to_all | solution.py:81
  160.6 8.5 collective-permute-start
  163.3 15.0 %all-to-all-start.3 = ((s32[64,1,6]{2,1,0:T(1,128)}), s32[64,1,6]{2,1,0:T(1,128)S(1)}, u32[]{:S(2)}, u32[]{:S(2)}) async-start(s32[64,1,6]{2,1,0:T(1,128)} %bitcast.21), calls=%async_computation.3 | async-start | bytes 65536 | tf_op jit(solution)/shard_map/all_to_all | solution.py:74
  178.9 56.2 %all-to-all-start.4 = ((bf16[64,6,2048]{2,1,0:T(8,128)(2,1)}), bf16[64,6,2048]{2,1,0:T(8,128)(2,1)S(1)}, u32[]{:S(2)}, u32[]{:S(2)}) async-start(bf16[64,6,2048]{2,1,0:T(8,128)(2,1)} %reshape.704), calls=%async_computation.4 | async-start | bytes 4194304 | tf_op jit(solution)/shard_map/all_to_all | solution.py:73
  249.6 10.5 copy-start.37
  249.6 57.2 %all-to-all-start.5 = ((bf16[64,6,2048]{2,1,0:T(8,128)(2,1)}), bf16[64,6,2048]{2,1,0:T(8,128)(2,1)}, u32[]{:S(2)}, u32[]{:S(2)}) async-start(bf16[64,6,2048]{2,1,0:T(8,128)(2,1)} %reshape.705), calls=%async_computation.5 | async-start | bytes 4194304 | tf_op jit(solution)/shard_map/all_to_all | solution.py:81
  313.3 8.8 collective-permute-start.1
  316.1 15.2 %all-to-all-start.6 = ((s32[64,1,6]{2,1,0:T(1,128)}), s32[64,1,6]{2,1,0:T(1,128)S(1)}, u32[]{:S(2)}, u32[]{:S(2)}) async-start(s32[64,1,6]{2,1,0:T(1,128)} %bitcast.32), calls=%async_computation.6 | async-start | bytes 65536 | tf_op jit(solution)/shard_map/all_to_all | solution.py:74
  331.9 56.2 %all-to-all-start.7 = ((bf16[64,6,2048]{2,1,0:T(8,128)(2,1)}), bf16[64,6,2048]{2,1,0:T(8,128)(2,1)S(1)}, u32[]{:S(2)}, u32[]{:S(2)}) async-start(bf16[64,6,2048]{2,1,0:T(8,128)(2,1)} %reshape.710), calls=%async_computation.7 | async-start | bytes 4194304 | tf_op jit(solution)/shard_map/all_to_all | solution.py:73
  402.5 57.3 %all-to-all-start.8 = ((bf16[64,6,2048]{2,1,0:T(8,128)(2,1)}), bf16[64,6,2048]{2,1,0:T(8,128)(2,1)}, u32[]{:S(2)}, u32[]{:S(2)}) async-start(bf16[64,6,2048]{2,1,0:T(8,128)(2,1)} %reshape.711), calls=%async_computation.8 | async-start | bytes 4194304 | tf_op jit(solution)/shard_map/all_to_all | solution.py:81
  466.4 8.4 collective-permute-start.2
  468.6 15.3 %all-to-all-start.9 = ((s32[64,1,6]{2,1,0:T(1,128)}), s32[64,1,6]{2,1,0:T(1,128)S(1)}, u32[]{:S(2)}, u32[]{:S(2)}) async-start(s32[64,1,6]{2,1,0:T(1,128)} %bitcast.43), calls=%async_computation.9 | async-start | bytes 65536 | tf_op jit(solution)/shard_map/all_to_all | solution.py:74
  484.5 56.1 %all-to-all-start.10 = ((bf16[64,6,2048]{2,1,0:T(8,128)(2,1)}), bf16[64,6,2048]{2,1,0:T(8,128)(2,1)S(1)}, u32[]{:S(2)}, u32[]{:S(2)}) async-start(bf16[64,6,2048]{2,1,0:T(8,128)(2,1)} %reshape.716), calls=%async_computation.10 | async-start | bytes 4194304 | tf_op jit(solution)/shard_map/all_to_all | solution.py:73
  555.1 10.5 %copy-start.39 = (f32[32]{0:T(128)S(1)}, f32[32]{0:T(128)}, u32[]{:S(2)}) copy-start(f32[32]{0:T(128)} %copy-done.38) | copy-start | bytes 388
  555.1 57.2 %all-to-all-start.11 = ((bf16[64,6,2048]{2,1,0:T(8,128)(2,1)}), bf16[64,6,2048]{2,1,0:T(8,128)(2,1)}, u32[]{:S(2)}, u32[]{:S(2)}) async-start(bf16[64,6,2048]{2,1,0:T(8,128)(2,1)} %reshape.717), calls=%async_computation.11 | async-start | bytes 4194304 | tf_op jit(solution)/shard_map/all_to_all | solution.py:81
  618.8 9.1 collective-permute-start.3
  621.6 15.5 %all-to-all-start.12 = ((s32[64,1,6]{2,1,0:T(1,128)}), s32[64,1,6]{2,1,0:T(1,128)S(1)}, u32[]{:S(2)}, u32[]{:S(2)}) async-start(s32[64,1,6]{2,1,0:T(1,128)} %bitcast.54), calls=%async_computation.12 | async-start | bytes 65536 | tf_op jit(solution)/shard_map/all_to_all | solution.py:74
  637.7 56.1 %all-to-all-start.13 = ((bf16[64,6,2048]{2,1,0:T(8,128)(2,1)}), bf16[64,6,2048]{2,1,0:T(8,128)(2,1)S(1)}, u32[]{:S(2)}, u32[]{:S(2)}) async-start(bf16[64,6,2048]{2,1,0:T(8,128)(2,1)} %reshape.722), calls=%async_computation.13 | async-start | bytes 4194304 | tf_op jit(solution)/shard_map/all_to_all | solution.py:73
  695.7 57.3 %all-to-all-start.14 = ((bf16[64,6,2048]{2,1,0:T(8,128)(2,1)}), bf16[64,6,2048]{2,1,0:T(8,128)(2,1)}, u32[]{:S(2)}, u32[]{:S(2)}) async-start(bf16[64,6,2048]{2,1,0:T(8,128)(2,1)} %reshape.723), calls=%async_computation.14 | async-start | bytes 4194304 | tf_op jit(solution)/shard_map/all_to_all | solution.py:81
  759.5 15.3 %collective-permute-start.4 = (bf16[32,2048]{1,0:T(8,128)(2,1)S(1)}, bf16[32,2048]{1,0:T(8,128)(2,1)S(1)}, u32[]{:S(2)}, u32[]{:S(2)}) collective-permute-start(bf16[32,2048]{1,0:T(8,128)(2,1)S(1)} %get-tuple-element.139), channel_id=1, source_target_pairs={{0,64},{64,128},{128,192},{1,65},{65,129},{129,193},{2,66},{66,130... | collective-permute-start | bytes 393224 | tf_op jit(solution)/shard_map/ppermute | solution.py:12
  768.7 15.3 %all-to-all-start.15 = ((s32[64,1,6]{2,1,0:T(1,128)}), s32[64,1,6]{2,1,0:T(1,128)S(1)}, u32[]{:S(2)}, u32[]{:S(2)}) async-start(s32[64,1,6]{2,1,0:T(1,128)} %bitcast.65), calls=%async_computation.15 | async-start | bytes 65536 | tf_op jit(solution)/shard_map/all_to_all | solution.py:74
  784.6 56.3 %all-to-all-start.16 = ((bf16[64,6,2048]{2,1,0:T(8,128)(2,1)}), bf16[64,6,2048]{2,1,0:T(8,128)(2,1)S(1)}, u32[]{:S(2)}, u32[]{:S(2)}) async-start(bf16[64,6,2048]{2,1,0:T(8,128)(2,1)} %reshape.728), calls=%async_computation.16 | async-start | bytes 4194304 | tf_op jit(solution)/shard_map/all_to_all | solution.py:73
  842.7 57.3 %all-to-all-start.17 = ((bf16[64,6,2048]{2,1,0:T(8,128)(2,1)}), bf16[64,6,2048]{2,1,0:T(8,128)(2,1)}, u32[]{:S(2)}, u32[]{:S(2)}) async-start(bf16[64,6,2048]{2,1,0:T(8,128)(2,1)} %reshape.729), calls=%async_computation.17 | async-start | bytes 4194304 | tf_op jit(solution)/shard_map/all_to_all | solution.py:81
  906.5 8.7 collective-permute-start.5
  909.1 15.3 %all-to-all-start.18 = ((s32[64,1,6]{2,1,0:T(1,128)}), s32[64,1,6]{2,1,0:T(1,128)S(1)}, u32[]{:S(2)}, u32[]{:S(2)}) async-start(s32[64,1,6]{2,1,0:T(1,128)} %bitcast.77), calls=%async_computation.18 | async-start | bytes 65536 | tf_op jit(solution)/shard_map/all_to_all | solution.py:74
  925.0 56.4 %all-to-all-start.19 = ((bf16[64,6,2048]{2,1,0:T(8,128)(2,1)}), bf16[64,6,2048]{2,1,0:T(8,128)(2,1)S(1)}, u32[]{:S(2)}, u32[]{:S(2)}) async-start(bf16[64,6,2048]{2,1,0:T(8,128)(2,1)} %reshape.734), calls=%async_computation.19 | async-start | bytes 4194304 | tf_op jit(solution)/shard_map/all_to_all | solution.py:73
  983.1 57.3 %all-to-all-start.20 = ((bf16[64,6,2048]{2,1,0:T(8,128)(2,1)}), bf16[64,6,2048]{2,1,0:T(8,128)(2,1)}, u32[]{:S(2)}, u32[]{:S(2)}) async-start(bf16[64,6,2048]{2,1,0:T(8,128)(2,1)} %reshape.735), calls=%async_computation.20 | async-start | bytes 4194304 | tf_op jit(solution)/shard_map/all_to_all | solution.py:81
  (41 other events, 193.5 us)
where the time goes:
time: 1060 us; the launch traced here: 1050 us
  waiting for transfers between devices  712 us (67%)
  starting transfers between devices  141 us (13%)
  local copies, waits for them, and re-layouts  105 us (10%)
  matrix products  54.9 us (5%)
  other arithmetic  27.7 us (3%)
    all_to_all x7, waiting for transfers between devices, on_device(): lax.all_to_all(slot_buffer, 'dp', split_axis=0, concat_axis=0, tiled=True)  338 us
    all_to_all x7, waiting for transfers between devices, on_device(): lax.all_to_all(expert_out, 'dp', split_axis=0, concat_axis=0, tiled=True)  328 us
    all_to_all x7, starting transfers between devices, on_device(): lax.all_to_all(live_slots, 'dp', split_axis=0, concat_axis=0, tiled=True)  49.5 us
    all_to_all x7, waiting for transfers between devices, on_device(): lax.all_to_all(live_slots, 'dp', split_axis=0, concat_axis=0, tiled=True)  46.3 us
    all_to_all x7, starting transfers between devices, on_device(): lax.all_to_all(expert_out, 'dp', split_axis=0, concat_axis=0, tiled=True)  42.6 us
    all_to_all x7, starting transfers between devices, on_device(): lax.all_to_all(slot_buffer, 'dp', split_axis=0, concat_axis=0, tiled=True)  33.9 us
    dot_general x4, matrix products, expert_rows(): jnp.dot(hidden, down_mat, preferred_element_type=jnp.float32)  26.8 us
    reshape x14, local copies, waits for them, and re-layouts, on_device(): returned.reshape(slot_count, model_width)[target]  26.5 us
  transfers between devices with their start and end apart: 27, of which 21 were waited for; matrix products, arithmetic and copies ran while one was open for 6% of the time, Pallas kernels for 0%

commit v1 on v0

v1 whole, which is shorter than its diff:
```python
import jax
import jax.numpy as jnp
from jax import lax
from jax.experimental import pallas as pl
from jax.experimental.pallas import tpu as pltpu
from jax.sharding import PartitionSpec as P

EPS = 1e-06
def mlp_kernel(x_ref, gu_ref, down_ref, out_ref, gu_buf, down_buf, act, gu_sems, down_sems):
    count, depth, _ = gu_ref.shape
    inner = down_ref.shape[1]
    ff = count * inner
    gu_copies = [
        pltpu.make_async_copy(gu_ref.at[j], gu_buf.at[j], gu_sems.at[j]) for j in range(count)
    ]
    down_copies = [
        pltpu.make_async_copy(
            down_ref.at[j], down_buf.at[pl.ds(j * inner, inner)], down_sems.at[j]
        )
        for j in range(count)
    ]
    for copy in gu_copies + down_copies:
        copy.start()
    for j in range(count):
        gu_copies[j].wait()
        part = jnp.dot(
            x_ref[:, j * depth : (j + 1) * depth], gu_buf[j], preferred_element_type=jnp.float32
        )
        if j == 0:
            act[...] = part
        else:
            act[...] += part
    gate_act, up_act = act[:, :ff], act[:, ff:]
    hidden = (gate_act / (1.0 + jnp.exp(-gate_act)) * up_act).astype(jnp.bfloat16)
    for copy in down_copies:
        copy.wait()
    out_ref[...] = jnp.dot(
        hidden, down_buf[...], preferred_element_type=jnp.float32
    ).astype(jnp.bfloat16)


def expert_mlp(rows, gate_up, down):
    count, depth, both = gate_up.shape
    row_count, width = rows.shape
    inner = down.shape[1]
    return pl.pallas_call(
        mlp_kernel,
        out_shape=jax.ShapeDtypeStruct((row_count, width), jnp.bfloat16),
        in_specs=[pl.BlockSpec(memory_space=pltpu.VMEM)]
        + [pl.BlockSpec(memory_space=pl.ANY)] * 2,
        out_specs=pl.BlockSpec(memory_space=pltpu.VMEM),
        scratch_shapes=[
            pltpu.VMEM((count, depth, both), jnp.bfloat16),
            pltpu.VMEM((count * inner, width), jnp.bfloat16),
            pltpu.VMEM((row_count, both), jnp.float32),
            pltpu.SemaphoreType.DMA((count,)),
            pltpu.SemaphoreType.DMA((count,)),
        ],
        compiler_params=pltpu.CompilerParams(vmem_limit_bytes=48 * 1024 * 1024),
    )(rows, gate_up, down)


def on_device(inputs, route, gain, router, w_gate, w_up, w_down):
    sections = lax.axis_size("section")
    section = lax.axis_index("section")
    micro_count, tok_rows, width = inputs.shape
    top_count = route.shape[-1]
    experts = router.shape[-1]
    capacity = min(2 * tok_rows * top_count // experts, tok_rows)
    slots = experts * capacity
    lanes = 128
    block = capacity * width // lanes

    gate_up = jnp.concatenate([w_gate[0, 0], w_up[0, 0]], axis=1)
    gate_up = gate_up.reshape(sections, width // sections, -1)
    down = w_down[0, 0].reshape(sections, -1, width)
    gate_up_parts = lax.all_to_all(gate_up, "section", 0, 0, tiled=True)
    down_parts = lax.all_to_all(down, "section", 0, 0, tiled=True)

    micro_route = lax.all_to_all(route[0], "section", 0, 0, tiled=True)
    small = jnp.concatenate([router[0], gain[0].reshape(-1, experts)], axis=0)
    small = lax.all_gather(small, "section", axis=0)
    gains = small[:, width:, :].reshape(sections, width).astype(jnp.float32)
    routers = small[:, :width, :]

    expert_ids = jnp.arange(experts, dtype=jnp.int32)
    named = jnp.sum(
        (micro_route[..., None] == expert_ids).astype(jnp.float32), axis=2
    )
    earlier = jnp.tril(jnp.ones((tok_rows, tok_rows), jnp.float32), -1)
    rank = jnp.einsum("ts,lse->lte", earlier, named)
    slot_of = jnp.arange(capacity, dtype=jnp.float32)
    chosen = jnp.where(
        (rank[..., None] == slot_of) & (named[..., None] > 0), 1.0, 0.0
    )
    chosen = chosen.reshape(sections, tok_rows, slots)

    state = lax.dynamic_index_in_dim(inputs, section, 0, keepdims=False)
    outs = []
    for layer in range(sections):
        wide = state.astype(jnp.float32)
        inv_rms = lax.rsqrt(jnp.mean(wide * wide, axis=1, keepdims=True) + EPS)
        normed = (wide * inv_rms * gains[layer]).astype(jnp.bfloat16)
        packed = lax.dot_general(
            chosen[layer].astype(jnp.bfloat16),
            normed,
            (((0,), (0,)), ((), ())),
            preferred_element_type=jnp.float32,
        ).astype(jnp.bfloat16)
        sent = packed.reshape(experts, block, lanes)
        arrived = lax.all_to_all(sent, "dp", 0, 0, tiled=True)
        logits = jnp.dot(normed, routers[layer], preferred_element_type=jnp.float32)
        scores = jax.nn.sigmoid(logits) * named[layer]
        weights = scores / jnp.sum(scores, axis=1, keepdims=True)
        mix = (jnp.repeat(weights, capacity, axis=1)) * chosen[layer]
        mix_high = lax.reduce_precision(mix, 8, 7)
        mix_pair = jnp.concatenate([mix_high, mix - mix_high], axis=0).astype(jnp.bfloat16)

        rows = arrived.reshape(slots, width)
        layer_gu = lax.all_gather(gate_up_parts[layer], "section", axis=0)
        layer_down = lax.all_gather(down_parts[layer], "section", axis=0)
        expert_out = expert_mlp(rows, layer_gu, layer_down)
        returned = lax.all_to_all(
            expert_out.reshape(experts, block, lanes), "dp", 0, 0, tiled=True
        ).reshape(slots, width)
        mixed = jnp.dot(mix_pair, returned, preferred_element_type=jnp.float32)
        state = (wide + (mixed[:tok_rows] + mixed[tok_rows:])).astype(jnp.bfloat16)
        outs.append(state)
    states = lax.all_to_all(jnp.stack(outs), "section", 0, 0, tiled=True)
    return states[None]


def solution(mesh):
    in_specs = (
        P(None, "dp", None),
        P("section", None, "dp", None),
        P("section", None),
        P("section", None, None),
        P("section", "dp", None, None),
        P("section", "dp", None, None),
        P("section", "dp", None, None),
    )
    out_specs = P("section", None, "dp", None)
    return jax.shard_map(
        on_device, mesh=mesh, in_specs=in_specs, out_specs=out_specs, check_vma=False
    )
```

time: 1060 us -> 660 us (0.62); the launches traced: 1050 us -> 659 us
  waiting for transfers between devices: 712 us -> 378 us
  blocking collectives: 0 us -> 104 us
  local copies, waits for them, and re-layouts: 105 us -> 35.3 us
  starting transfers between devices: 141 us -> 78.7 us
  matrix products: 54.9 us -> 12.9 us
  Pallas kernels: 0 us -> 23.1 us
  other arithmetic: 27.7 us -> 13.5 us
    all_to_all x21 -> x9, waiting for transfers between devices: 712 us -> 358 us  [the longest x4 146 us: on_device(): lax.all_to_all(expert_out.reshape(experts, block, lanes), 'dp', 0, 0, til...]
    all_to_all x0 -> x3, blocking collectives: none -> 104 us  [the longest x2 91.4 us: on_device(): arrived = lax.all_to_all(sent, 'dp', 0, 0, tiled=True)]
    all_to_all x21 -> x9, starting transfers between devices: 126 us -> 78.4 us  [the longest x4 41.3 us: on_device(): lax.all_to_all(expert_out.reshape(experts, block, lanes), 'dp', 0, 0, til...]
    dot_general x29 -> x13, matrix products: 54.9 us -> 12.9 us  [the longest x4 5.46 us: on_device(): logits = jnp.dot(normed, routers[layer], preferred_element_type=jnp.float32)]
    reshape x32 -> x20, local copies, waits for them, and re-layouts: 54.6 us -> 20.1 us  [the longest x4 8.54 us: on_device(): expert_out.reshape(experts, block, lanes)]
    gather x42 -> x0, local copies, waits for them, and re-layouts: 27.2 us -> none  [the longest x35 13.9 us: on_device(): scores = jax.nn.sigmoid(jnp.take_along_axis(logits, chosen_ids, axis=1))]
    pallas_call x0 -> x4, Pallas kernels: none -> 23.1 us  [expert_mlp(): pl.pallas_call(mlp_kernel, out_shape=jax.ShapeDtypeStruct((row_count, wid...]
    all_gather x0 -> x9, waiting for transfers between devices: none -> 16.4 us  [the longest x4 16.3 us: on_device(): layer_gu = lax.all_gather(gate_up_parts[layer], 'section', axis=0)]
  transfers between devices with their start and end apart: 27 -> 18, of which waited for: 21 -> 12; matrix products, arithmetic and copies ran while one was open for 6% -> 8% of each run, Pallas kernels for 0% -> 3%
where the time goes in v1:
time: 660 us; the launch traced here: 659 us
  waiting for transfers between devices  378 us (57%)
  blocking collectives  104 us (16%)
  starting transfers between devices  78.7 us (12%)
  local copies, waits for them, and re-layouts  35.3 us (5%)
  Pallas kernels  23.1 us (4%)
  between operations  13.9 us (2%)
  other arithmetic  13.5 us (2%)
  matrix products  12.9 us (2%)
    all_to_all x4, waiting for transfers between devices, on_device(): lax.all_to_all(expert_out.reshape(experts, block, lanes), 'dp', 0, 0, til...  146 us
    all_to_all x1, waiting for transfers between devices, on_device(): gate_up_parts = lax.all_to_all(gate_up, 'section', 0, 0, tiled=True)  92 us
    all_to_all x2, blocking collectives, on_device(): arrived = lax.all_to_all(sent, 'dp', 0, 0, tiled=True)  91.4 us
    all_to_all x2, waiting for transfers between devices, on_device(): arrived = lax.all_to_all(sent, 'dp', 0, 0, tiled=True)  78.1 us
    all_to_all x4, starting transfers between devices, on_device(): lax.all_to_all(expert_out.reshape(experts, block, lanes), 'dp', 0, 0, til...  41.3 us
    all_to_all x1, waiting for transfers between devices, on_device(): down_parts = lax.all_to_all(down, 'section', 0, 0, tiled=True)  37.7 us
    all_to_all x2, starting transfers between devices, on_device(): arrived = lax.all_to_all(sent, 'dp', 0, 0, tiled=True)  23.4 us
    pallas_call x4, Pallas kernels, expert_mlp(): pl.pallas_call(mlp_kernel, out_shape=jax.ShapeDtypeStruct((row_count, wid...  23.1 us
  transfers between devices with their start and end apart: 18, of which 12 were waited for; matrix products, arithmetic and copies ran while one was open for 8% of the time, Pallas kernels for 3%

profile of v1, /device:TPU:1, one launch (start us, length us, event | category | flops | bytes accessed | tf_op | source)
XLA Modules:
  0.0 659.2 jit_solution(16214061599012433561)
XLA Ops:
  6.5 5.1 all-to-all-start.3
  12.7 6.0 pad_maximum_fusion
  18.6 37.7 %all-to-all-done.3 = bf16[4,192,2048]{2,1,0:T(8,128)(2,1)S(1)} async-done(((bf16[4,192,2048]{2,1,0:T(8,128)(2,1)}), bf16[4,192,2048]{2,1,0:T(8,128)(2,1)S(1)}, u32[]{:S(2)}, u32[]{:S(2)}) %all-to-all-start.3) | async-done | bytes 3145760 | tf_op jit(solution)/shard_map/all_to_all | solution.py:78
  56.3 5.3 all-to-all-start.2
  63.5 92.0 %all-to-all-done.2 = bf16[4,512,1536]{2,1,0:T(8,128)(2,1)} async-done(((bf16[4,512,1536]{2,1,0:T(8,128)(2,1)}), bf16[4,512,1536]{2,1,0:T(8,128)(2,1)}, u32[]{:S(2)}, u32[]{:S(2)}) %all-to-all-start.2) | async-done | bytes 6291488 | tf_op jit(solution)/shard_map/all_to_all | solution.py:77
  155.4 5.5 fusion.85
  163.4 3.2 all-to-all-start
  166.9 3.9 all-to-all-done
  178.4 17.3 %all-to-all-start.1 = ((bf16[64,96,128]{2,1,0:T(8,128)(2,1)}), bf16[64,96,128]{2,1,0:T(8,128)(2,1)S(1)}, u32[]{:S(2)}, u32[]{:S(2)}) async-start(bf16[64,96,128]{2,1,0:T(8,128)(2,1)} %reshape.158), calls=%async_computation.1 | async-start | bytes 3145728 | tf_op jit(solution)/shard_map/all_to_all | solution.py:111
  196.5 39.0 %all-to-all-done.1 = bf16[64,96,128]{2,1,0:T(8,128)(2,1)S(1)} async-done(((bf16[64,96,128]{2,1,0:T(8,128)(2,1)}), bf16[64,96,128]{2,1,0:T(8,128)(2,1)S(1)}, u32[]{:S(2)}, u32[]{:S(2)}) %all-to-all-start.1) | async-done | bytes 1572896 | tf_op jit(solution)/shard_map/all_to_all | solution.py:111
  236.3 5.8 shard_map.73
  242.1 2.1 reshape.160
  244.3 8.8 %all-to-all-start.4 = ((bf16[64,96,128]{2,1,0:T(8,128)(2,1)}), bf16[64,96,128]{2,1,0:T(8,128)(2,1)S(1)}, u32[]{:S(2)}, u32[]{:S(2)}) async-start(bf16[64,96,128]{2,1,0:T(8,128)(2,1)} %reshape.160), calls=%async_computation.4 | async-start | bytes 3145728 | tf_op jit(solution)/shard_map/all_to_all | solution.py:123
  256.6 36.3 %all-to-all-done.4 = bf16[64,96,128]{2,1,0:T(8,128)(2,1)S(1)} async-done(((bf16[64,96,128]{2,1,0:T(8,128)(2,1)}), bf16[64,96,128]{2,1,0:T(8,128)(2,1)S(1)}, u32[]{:S(2)}, u32[]{:S(2)}) %all-to-all-start.4) | async-done | bytes 1572896 | tf_op jit(solution)/shard_map/all_to_all | solution.py:123
  297.6 45.7 %all_to_all.60 = bf16[64,96,128]{2,1,0:T(8,128)(2,1)S(1)} all-to-all(bf16[64,96,128]{2,1,0:T(8,128)(2,1)S(1)} %reshape.163), channel_id=1, replica_groups=mesh['section'=4,'dp'=64] {'dp'}, dimensions={0} | all-to-all | bytes 3145728 | tf_op jit(solution)/shard_map/all_to_all | solution.py:111
  344.0 4.9 all-gather.16.cloned.1.call-done.gu_ref
  349.0 5.8 shard_map.74
  354.8 2.1 reshape.165
  356.9 10.8 %all-to-all-start.6 = ((bf16[64,96,128]{2,1,0:T(8,128)(2,1)}), bf16[64,96,128]{2,1,0:T(8,128)(2,1)S(1)}, u32[]{:S(2)}, u32[]{:S(2)}) async-start(bf16[64,96,128]{2,1,0:T(8,128)(2,1)} %reshape.165), calls=%async_computation.6 | async-start | bytes 3145728 | tf_op jit(solution)/shard_map/all_to_all | solution.py:123
  371.7 35.9 %all-to-all-done.6 = bf16[64,96,128]{2,1,0:T(8,128)(2,1)S(1)} async-done(((bf16[64,96,128]{2,1,0:T(8,128)(2,1)}), bf16[64,96,128]{2,1,0:T(8,128)(2,1)S(1)}, u32[]{:S(2)}, u32[]{:S(2)}) %all-to-all-start.6) | async-done | bytes 1572896 | tf_op jit(solution)/shard_map/all_to_all | solution.py:123
  412.0 6.1 all-to-all-start.7
  418.8 39.1 %all-to-all-done.7 = bf16[64,96,128]{2,1,0:T(8,128)(2,1)S(1)} async-done(((bf16[64,96,128]{2,1,0:T(8,128)(2,1)}), bf16[64,96,128]{2,1,0:T(8,128)(2,1)S(1)}, u32[]{:S(2)}, u32[]{:S(2)}) %all-to-all-start.7) | async-done | bytes 1572896 | tf_op jit(solution)/shard_map/all_to_all | solution.py:111
  458.6 5.2 all-gather.20.cloned.1.call-done.gu_ref
  463.8 5.8 shard_map.75
  471.7 10.8 %all-to-all-start.8 = ((bf16[64,96,128]{2,1,0:T(8,128)(2,1)}), bf16[64,96,128]{2,1,0:T(8,128)(2,1)S(1)}, u32[]{:S(2)}, u32[]{:S(2)}) async-start(bf16[64,96,128]{2,1,0:T(8,128)(2,1)} %reshape.170), calls=%async_computation.8 | async-start | bytes 3145728 | tf_op jit(solution)/shard_map/all_to_all | solution.py:123
  485.7 36.6 %all-to-all-done.8 = bf16[64,96,128]{2,1,0:T(8,128)(2,1)S(1)} async-done(((bf16[64,96,128]{2,1,0:T(8,128)(2,1)}), bf16[64,96,128]{2,1,0:T(8,128)(2,1)S(1)}, u32[]{:S(2)}, u32[]{:S(2)}) %all-to-all-start.8) | async-done | bytes 1572896 | tf_op jit(solution)/shard_map/all_to_all | solution.py:123
  526.1 45.7 %all_to_all.61 = bf16[64,96,128]{2,1,0:T(8,128)(2,1)S(1)} all-to-all(bf16[64,96,128]{2,1,0:T(8,128)(2,1)S(1)} %reshape.173), channel_id=1, replica_groups=mesh['section'=4,'dp'=64] {'dp'}, dimensions={0} | all-to-all | bytes 3145728 | tf_op jit(solution)/shard_map/all_to_all | solution.py:111
  572.5 6.2 all-gather.24.cloned.1.call-done.gu_ref
  578.7 5.8 shard_map.76
  586.6 10.8 %all-to-all-start.10 = ((bf16[64,96,128]{2,1,0:T(8,128)(2,1)}), bf16[64,96,128]{2,1,0:T(8,128)(2,1)S(1)}, u32[]{:S(2)}, u32[]{:S(2)}) async-start(bf16[64,96,128]{2,1,0:T(8,128)(2,1)} %reshape.175), calls=%async_computation.10 | async-start | bytes 3145728 | tf_op jit(solution)/shard_map/all_to_all | solution.py:123
  599.8 37.5 %all-to-all-done.10 = bf16[64,96,128]{2,1,0:T(8,128)(2,1)S(1)} async-done(((bf16[64,96,128]{2,1,0:T(8,128)(2,1)}), bf16[64,96,128]{2,1,0:T(8,128)(2,1)S(1)}, u32[]{:S(2)}, u32[]{:S(2)}) %all-to-all-start.10) | async-done | bytes 1572896 | tf_op jit(solution)/shard_map/all_to_all | solution.py:123
  639.5 12.3 %all_to_all.62 = bf16[4,32,2048]{2,1,0:T(8,128)(2,1)S(1)} all-to-all(bf16[4,32,2048]{2,1,0:T(8,128)(2,1)S(1)} %pad_maximum_fusion.1), channel_id=1, replica_groups=mesh['section'=4,'dp'=64] {'section'}, dimensions={0} | all-to-all | bytes 1048576 | tf_op jit(solution)/shard_map/all_to_all | solution.py:129
  (157 shorter events, 50.0 us)
Async XLA Ops:
  6.5 5.2 copy-start.18
  6.5 5.4 copy-start.13
  6.5 49.8 %all-to-all-start.3 = ((bf16[4,192,2048]{2,1,0:T(8,128)(2,1)}), bf16[4,192,2048]{2,1,0:T(8,128)(2,1)S(1)}, u32[]{:S(2)}, u32[]{:S(2)}) async-start(bf16[4,192,2048]{2,1,0:T(8,128)(2,1)} %bitcast.103), calls=%async_computation.3 | async-start | bytes 6291456 | tf_op jit(solution)/shard_map/all_to_all | solution.py:78
  11.7 162.4 %all-gather.28.cloned.1.call-start = ((), (), s32[]{:S(2)}) async-start(), calls=%async_computation.20 | async-start | bytes 1392640 | tf_op jit(solution)/shard_map/all_gather | solution.py:82
  56.3 99.1 %all-to-all-start.2 = ((bf16[4,512,1536]{2,1,0:T(8,128)(2,1)}), bf16[4,512,1536]{2,1,0:T(8,128)(2,1)}, u32[]{:S(2)}, u32[]{:S(2)}) async-start(bf16[4,512,1536]{2,1,0:T(8,128)(2,1)} %pad_maximum_fusion), calls=%async_computation.2 | async-start | bytes 12582912 | tf_op jit(solution)/shard_map/all_to_all | solution.py:77
  61.6 174.7 %all-gather.14.cloned.1.call-start = ((), (), s32[]{:S(2)}) async-start(), calls=%async_computation.13 | async-start | bytes 3932160 | tf_op jit(solution)/shard_map/all_gather | solution.py:121
  63.4 172.9 %all-gather.12.cloned.1.call-start = ((), (), s32[]{:S(2)}) async-start(), calls=%async_computation.12 | async-start | bytes 7864320 | tf_op jit(solution)/shard_map/all_gather | solution.py:120
  161.0 183.0 %all-gather.18.cloned.1.call-start = ((), (), s32[]{:S(2)}) async-start(), calls=%async_computation.15 | async-start | bytes 3932160 | tf_op jit(solution)/shard_map/all_gather | solution.py:121
  161.0 5.6 copy-start.12
  161.6 187.4 %all-gather.16.cloned.1.call-start = ((), (), s32[]{:S(2)}) async-start(), calls=%async_computation.14 | async-start | bytes 7864320 | tf_op jit(solution)/shard_map/all_gather | solution.py:120
  162.2 296.5 %all-gather.22.cloned.1.call-start = ((), (), s32[]{:S(2)}) async-start(), calls=%async_computation.17 | async-start | bytes 3932160 | tf_op jit(solution)/shard_map/all_gather | solution.py:121
  163.4 7.4 %all-to-all-start = ((s32[4,1,192]{2,1,0:T(1,128)}), s32[4,1,192]{2,1,0:T(1,128)S(1)}, u32[]{:S(2)}, u32[]{:S(2)}) async-start(s32[4,1,192]{2,1,0:T(1,128)} %reshape.184), calls=%async_computation | async-start | bytes 8192 | tf_op jit(solution)/shard_map/all_to_all | solution.py:80
  172.2 311.1 %copy-start.8 = (f32[4,32,64]{2,1,0:T(8,128)}, f32[4,32,64]{2,1,0:T(8,128)S(1)}, u32[]{:S(2)}) copy-start(f32[4,32,64]{2,1,0:T(8,128)S(1)} %convert_reduce_fusion) | copy-start | bytes 98308
  178.4 57.1 %all-to-all-start.1 = ((bf16[64,96,128]{2,1,0:T(8,128)(2,1)}), bf16[64,96,128]{2,1,0:T(8,128)(2,1)S(1)}, u32[]{:S(2)}, u32[]{:S(2)}) async-start(bf16[64,96,128]{2,1,0:T(8,128)(2,1)} %reshape.158), calls=%async_computation.1 | async-start | bytes 3145728 | tf_op jit(solution)/shard_map/all_to_all | solution.py:111
  195.8 268.0 %all-gather.20.cloned.1.call-start = ((), (), s32[]{:S(2)}) async-start(), calls=%async_computation.16 | async-start | bytes 7864320 | tf_op jit(solution)/shard_map/all_gather | solution.py:120
  244.3 8.8 %copy-start.1 = (f32[4,32,64,6]{1,3,2,0:T(8,128)S(1)}, f32[4,32,64,6]{1,3,2,0:T(8,128)}, u32[]{:S(2)}) copy-start(f32[4,32,64,6]{1,3,2,0:T(8,128)} %copy-done) | copy-start | bytes 589828
  244.3 48.6 %all-to-all-start.4 = ((bf16[64,96,128]{2,1,0:T(8,128)(2,1)}), bf16[64,96,128]{2,1,0:T(8,128)(2,1)S(1)}, u32[]{:S(2)}, u32[]{:S(2)}) async-start(bf16[64,96,128]{2,1,0:T(8,128)(2,1)} %reshape.160), calls=%async_computation.4 | async-start | bytes 3145728 | tf_op jit(solution)/shard_map/all_to_all | solution.py:123
  256.6 37.1 %copy-start.9 = (bf16[32,384]{0,1:T(8,128)(2,1)S(1)}, bf16[32,384]{0,1:T(8,128)(2,1)}, u32[]{:S(2)}) copy-start(bf16[32,384]{0,1:T(8,128)(2,1)} %get-tuple-element.29) | copy-start | bytes 73732
  356.9 11.6 %copy-start.7 = (f32[1,32,64,6]{1,3,2,0:T(8,128)S(1)}, f32[1,32,64,6]{1,3,2,0:T(8,128)}, u32[]{:S(2)}) copy-start(f32[1,32,64,6]{1,3,2,0:T(8,128)} %get-tuple-element.21) | copy-start | bytes 147460
  356.9 12.3 %copy-start.15 = (f32[1,32,64]{1,2,0:T(8,128)S(1)}, f32[1,32,64]{1,2,0:T(8,128)}, u32[]{:S(2)}) copy-start(f32[1,32,64]{1,2,0:T(8,128)} %get-tuple-element.32) | copy-start | bytes 24580
  356.9 12.4 %copy-start.20 = (f32[32]{0:T(128)S(1)}, f32[32]{0:T(128)}, u32[]{:S(2)}) copy-start(f32[32]{0:T(128)} %copy-done.19) | copy-start | bytes 388
  356.9 50.6 %all-to-all-start.6 = ((bf16[64,96,128]{2,1,0:T(8,128)(2,1)}), bf16[64,96,128]{2,1,0:T(8,128)(2,1)S(1)}, u32[]{:S(2)}, u32[]{:S(2)}) async-start(bf16[64,96,128]{2,1,0:T(8,128)(2,1)} %reshape.165), calls=%async_computation.6 | async-start | bytes 3145728 | tf_op jit(solution)/shard_map/all_to_all | solution.py:123
  367.7 204.8 %all-gather.26.cloned.1.call-start = ((), (), s32[]{:S(2)}) async-start(), calls=%async_computation.19 | async-start | bytes 3932160 | tf_op jit(solution)/shard_map/all_gather | solution.py:121
  371.6 36.6 %copy-start.10 = (bf16[32,384]{0,1:T(8,128)(2,1)S(1)}, bf16[32,384]{0,1:T(8,128)(2,1)}, u32[]{:S(2)}) copy-start(bf16[32,384]{0,1:T(8,128)(2,1)} %get-tuple-element.27) | copy-start | bytes 73732
  371.7 36.6 %copy-start.11 = (bf16[32,384]{0,1:T(8,128)(2,1)S(1)}, bf16[32,384]{0,1:T(8,128)(2,1)}, u32[]{:S(2)}) copy-start(bf16[32,384]{0,1:T(8,128)(2,1)} %get-tuple-element.28) | copy-start | bytes 73732
  412.0 45.9 %all-to-all-start.7 = ((bf16[64,96,128]{2,1,0:T(8,128)(2,1)}), bf16[64,96,128]{2,1,0:T(8,128)(2,1)S(1)}, u32[]{:S(2)}, u32[]{:S(2)}) async-start(bf16[64,96,128]{2,1,0:T(8,128)(2,1)} %reshape.168), calls=%async_computation.7 | async-start | bytes 3145728 | tf_op jit(solution)/shard_map/all_to_all | solution.py:111
  418.1 160.6 %all-gather.24.cloned.1.call-start = ((), (), s32[]{:S(2)}) async-start(), calls=%async_computation.18 | async-start | bytes 7864320 | tf_op jit(solution)/shard_map/all_gather | solution.py:120
  471.7 10.9 %copy-start.6 = (f32[1,32,64,6]{1,3,2,0:T(8,128)S(1)}, f32[1,32,64,6]{1,3,2,0:T(8,128)}, u32[]{:S(2)}) copy-start(f32[1,32,64,6]{1,3,2,0:T(8,128)} %get-tuple-element.20) | copy-start | bytes 147460
  471.7 11.6 %copy-start.14 = (f32[1,32,64]{1,2,0:T(8,128)S(1)}, f32[1,32,64]{1,2,0:T(8,128)}, u32[]{:S(2)}) copy-start(f32[1,32,64]{1,2,0:T(8,128)} %get-tuple-element.31) | copy-start | bytes 24580
  471.7 50.6 %all-to-all-start.8 = ((bf16[64,96,128]{2,1,0:T(8,128)(2,1)}), bf16[64,96,128]{2,1,0:T(8,128)(2,1)S(1)}, u32[]{:S(2)}, u32[]{:S(2)}) async-start(bf16[64,96,128]{2,1,0:T(8,128)(2,1)} %reshape.170), calls=%async_computation.8 | async-start | bytes 3145728 | tf_op jit(solution)/shard_map/all_to_all | solution.py:123
  586.6 12.4 %copy-start.5 = (f32[32,384]{0,1:T(8,128)S(1)}, f32[32,384]{0,1:T(8,128)}, u32[]{:S(2)}) copy-start(f32[32,384]{0,1:T(8,128)} %squeeze.63) | copy-start | bytes 147460
  586.6 50.6 %all-to-all-start.10 = ((bf16[64,96,128]{2,1,0:T(8,128)(2,1)}), bf16[64,96,128]{2,1,0:T(8,128)(2,1)S(1)}, u32[]{:S(2)}, u32[]{:S(2)}) async-start(bf16[64,96,128]{2,1,0:T(8,128)(2,1)} %reshape.175), calls=%async_computation.10 | async-start | bytes 3145728 | tf_op jit(solution)/shard_map/all_to_all | solution.py:123
  (7 other events, 10.9 us)
Sparse Core Ops, SparseCore 0:
  14.3 37.8 all-gather.27
  64.3 72.7 all-gather.13
  161.1 73.1 all-gather.11
  236.0 42.8 all-gather.17
  280.5 68.4 all-gather.15
  350.6 42.8 all-gather.21
  395.3 68.4 all-gather.19
  465.6 42.8 all-gather.25
  510.3 68.4 all-gather.23

commit v2 on v1

v2 whole, which is shorter than its diff:
```python
import jax
import jax.numpy as jnp
from jax import lax
from jax.experimental import pallas as pl
from jax.experimental.pallas import tpu as pltpu
from jax.sharding import PartitionSpec as P

EPS = 1e-06
LANES = 128
VMEM_LIMIT = 48 * 1024 * 1024


def normalise(wide, gain_row):
    inv_rms = lax.rsqrt(jnp.mean(wide * wide, axis=1, keepdims=True) + EPS)
    return (wide * inv_rms * gain_row).astype(jnp.bfloat16)


def pack_rows(picker, normed, sent_ref):
    rows = jnp.dot(picker, normed, preferred_element_type=jnp.float32)
    sent_ref[...] = rows.astype(jnp.bfloat16).reshape(sent_ref.shape)


def first_kernel(state_ref, gain_ref, picker_ref, normed_ref, sent_ref):
    normed = normalise(state_ref[...].astype(jnp.float32), gain_ref[...])
    normed_ref[...] = normed
    pack_rows(picker_ref[...], normed, sent_ref)


def mix_rows(returned_ref, mix_ref, state_ref):
    tok_rows, width = state_ref.shape
    rows = returned_ref[...].reshape(returned_ref.shape[0], width)
    mixed = jnp.dot(mix_ref[...], rows, preferred_element_type=jnp.float32)
    total = state_ref[...].astype(jnp.float32) + (mixed[:tok_rows] + mixed[tok_rows:])
    return total.astype(jnp.bfloat16)


def step_kernel(
    returned_ref, mix_ref, state_ref, gain_ref, picker_ref, next_ref, normed_ref, sent_ref
):
    state = mix_rows(returned_ref, mix_ref, state_ref)
    next_ref[...] = state
    normed = normalise(state.astype(jnp.float32), gain_ref[...])
    normed_ref[...] = normed
    pack_rows(picker_ref[...], normed, sent_ref)


def last_kernel(returned_ref, mix_ref, state_ref, next_ref):
    next_ref[...] = mix_rows(returned_ref, mix_ref, state_ref)


def mlp_kernel(split, x_ref, *refs):
    sources = refs[:-4]
    out_ref, held, act, sems = refs[-4:]
    count, depth, both = held.shape
    ff = both // 2
    top = x_ref.shape[1] * x_ref.shape[2] // count
    tall = depth - top
    copies = []
    for part in range(count):
        source = sources[part] if split else sources[0].at[part]
        for place, (start, size) in enumerate(((0, top), (top, tall))):
            copies.append(
                pltpu.make_async_copy(
                    source.at[pl.ds(start, size)],
                    held.at[part, pl.ds(start, size)],
                    sems.at[place, part],
                )
            )
    top_copies, tall_copies = copies[::2], copies[1::2]
    for copy in top_copies + tall_copies:
        copy.start()
    rows = x_ref[...].reshape(x_ref.shape[0], count * top)
    for part in range(count):
        top_copies[part].wait()
        term = jnp.dot(
            rows[:, part * top : (part + 1) * top],
            held[part, :top, :],
            preferred_element_type=jnp.float32,
        )
        if part == 0:
            act[...] = term
        else:
            act[...] += term
    gate_act, up_act = act[:, :ff], act[:, ff:]
    hidden = (gate_act / (1.0 + jnp.exp(-gate_act)) * up_act).astype(jnp.bfloat16)
    outs = []
    for part in range(count):
        tall_copies[part].wait()
        total = None
        for k in range(ff // tall):
            term = jnp.dot(
                hidden[:, k * tall : (k + 1) * tall],
                held[part, top:, k * top : (k + 1) * top],
                preferred_element_type=jnp.float32,
            )
            total = term if total is None else total + term
        outs.append(total.astype(jnp.bfloat16))
    out_ref[...] = jnp.concatenate(outs, axis=1).reshape(out_ref.shape)


def expert_mlp(rows, sources):
    split = len(sources) > 1
    depth, both = sources[0].shape[-2:]
    count = len(sources) if split else sources[0].shape[0]
    return pl.pallas_call(
        lambda *refs: mlp_kernel(split, *refs),
        out_shape=jax.ShapeDtypeStruct(rows.shape, jnp.bfloat16),
        in_specs=[pl.BlockSpec(memory_space=pltpu.VMEM)]
        + [pl.BlockSpec(memory_space=pl.ANY)] * len(sources),
        out_specs=pl.BlockSpec(memory_space=pltpu.VMEM),
        scratch_shapes=[
            pltpu.VMEM((count, depth, both), jnp.bfloat16),
            pltpu.VMEM((rows.shape[0], both), jnp.float32),
            pltpu.SemaphoreType.DMA((2, count)),
        ],
        compiler_params=pltpu.CompilerParams(vmem_limit_bytes=VMEM_LIMIT),
    )(rows, *sources)


def lay_kernel(first_ref, gate_ref, up_ref, down_ref, *out_refs):
    top, ff = gate_ref.shape
    tall = out_refs[0].shape[0] - top
    for place, ref in enumerate(out_refs):

        @pl.when(pl.program_id(0) == place)
        def _(ref=ref):
            ref[:top, :ff] = gate_ref[...]
            ref[:top, ff:] = up_ref[...]
            for k in range(ff // tall):
                ref[top:, k * top : (k + 1) * top] = down_ref[k * tall : (k + 1) * tall, :]


def lay_out(first, gate, up, down, count):
    width, ff = gate.shape
    top = width // count
    depth = top + ff * top // (2 * ff)

    def pick(i, first_ref):
        return lax.rem(first_ref[0] + i, count)

    out = jax.ShapeDtypeStruct((depth, 2 * ff), jnp.bfloat16)
    grid_spec = pltpu.PrefetchScalarGridSpec(
        num_scalar_prefetch=1,
        grid=(count,),
        in_specs=[
            pl.BlockSpec((top, ff), lambda i, first_ref: (pick(i, first_ref), 0)),
            pl.BlockSpec((top, ff), lambda i, first_ref: (pick(i, first_ref), 0)),
            pl.BlockSpec((ff, top), lambda i, first_ref: (0, pick(i, first_ref))),
        ],
        out_specs=[
            pl.BlockSpec((depth, 2 * ff), lambda i, first_ref: (0, 0)) for _ in range(count)
        ],
    )
    return pl.pallas_call(
        lay_kernel,
        grid_spec=grid_spec,
        out_shape=[out] * count,
        compiler_params=pltpu.CompilerParams(vmem_limit_bytes=VMEM_LIMIT),
    )(first.reshape(1).astype(jnp.int32), gate, up, down)


def after(values, *tokens):
    return lax.optimization_barrier((values, tokens))[0]


def on_device(inputs, route, gain, router, w_gate, w_up, w_down):
    sections = lax.axis_size("section")
    section = lax.axis_index("section")
    micro_count, tok_rows, width = inputs.shape
    top_count = route.shape[-1]
    experts = router.shape[-1]
    ff = w_gate.shape[-1]
    capacity = min(2 * tok_rows * top_count // experts, tok_rows)
    slots = experts * capacity
    tiles = width // LANES
    rows_shape = jax.ShapeDtypeStruct((slots, tiles, LANES), jnp.bfloat16)
    tok_shape = jax.ShapeDtypeStruct((tok_rows, width), jnp.bfloat16)
    params = pltpu.CompilerParams(vmem_limit_bytes=VMEM_LIMIT)

    def shifted(part, by):
        return lax.ppermute(
            part, "section", [(i, (i + by) % sections) for i in range(sections)]
        )

    route_values = route[0].reshape(micro_count, -1).astype(jnp.bfloat16)
    route_size = route_values.shape[1]
    padding = -route_size % LANES
    route_values = jnp.pad(route_values, ((0, 0), (0, padding)))
    gain_values = jnp.broadcast_to(gain[0].reshape(1, tiles, LANES), (sections, tiles, LANES))
    brief = jnp.concatenate(
        [gain_values, route_values.reshape(micro_count, -1, LANES)], axis=1
    )
    brief = lax.all_to_all(brief, "section", 0, 0, tiled=True)
    gains = brief[:, :tiles].reshape(sections, 1, width).astype(jnp.float32)
    micro_route = brief[:, tiles:].reshape(sections, -1)[:, :route_size]
    micro_route = micro_route.reshape(sections, tok_rows, top_count).astype(jnp.int32)

    laid = lay_out(section, w_gate[0, 0], w_up[0, 0], w_down[0, 0], sections)
    parts = [laid[0]] + [shifted(laid[by], by) for by in range(1, sections)]

    def own_part(layer, held):
        return lax.select_n(lax.rem(section + sections - layer, sections), *held)

    first_part = own_part(0, parts)
    gathered = [lax.all_gather(first_part, "section", axis=0)]

    dp_count = lax.axis_size("dp")
    core = lax.rem(lax.axis_index("dp"), 2)
    router_half = lax.dynamic_slice_in_dim(router[0], core * (width // 2), width // 2, 0)
    router_half = after(router_half.reshape(-1, LANES), first_part)
    router_halves = [router_half] + [shifted(router_half, by) for by in range(1, sections)]
    own_halves = jnp.stack([own_part(layer, router_halves) for layer in range(sections)])
    other_halves = lax.ppermute(
        own_halves, "dp", [(i, i + 1 - 2 * (i % 2)) for i in range(dp_count)]
    )
    router_pair = jnp.where(core == 0, own_halves, other_halves), jnp.where(
        core == 0, other_halves, own_halves
    )
    routers = jnp.concatenate(router_pair, axis=1).reshape(sections, width, experts)

    expert_ids = jnp.arange(experts, dtype=jnp.int32)
    named = jnp.sum(
        (micro_route[..., None] == expert_ids).astype(jnp.float32), axis=2
    )
    earlier = jnp.tril(jnp.ones((tok_rows, tok_rows), jnp.float32), -1)
    rank = jnp.einsum("ts,lse->lte", earlier, named)
    slot_of = jnp.arange(capacity, dtype=jnp.float32)
    chosen = jnp.where(
        (rank[..., None] == slot_of) & (named[..., None] > 0), 1.0, 0.0
    )
    chosen = chosen.reshape(sections, tok_rows, slots)
    pickers = jnp.swapaxes(chosen, 1, 2).astype(jnp.bfloat16)

    def across(rows):
        blocks = rows.reshape(experts, capacity * tiles, LANES)
        moved = lax.all_to_all(blocks, "dp", 0, 0, tiled=True)
        return moved.reshape(slots, tiles, LANES)

    state = lax.dynamic_index_in_dim(inputs, section, 0, keepdims=False)
    state = after(state, first_part)
    normed, sent = pl.pallas_call(
        first_kernel, out_shape=[tok_shape, rows_shape], compiler_params=params
    )(state, gains[0], pickers[0])
    outs = []
    for layer in range(sections):
        arrived = across(sent)
        logits = jnp.dot(normed, routers[layer], preferred_element_type=jnp.float32)
        scores = jax.nn.sigmoid(logits) * named[layer]
        weights = scores / jnp.sum(scores, axis=1, keepdims=True)
        mix = (jnp.repeat(weights, capacity, axis=1)) * chosen[layer]
        mix_high = lax.reduce_precision(mix, 8, 7)
        mix_pair = jnp.concatenate([mix_high, mix - mix_high], axis=0).astype(jnp.bfloat16)

        if layer == 0:
            held = after(parts, arrived)
            for later in range(1, sections):
                part = own_part(later, held)
                gathered.append(lax.all_gather(part, "section", axis=0))
        expert_out = expert_mlp(arrived, [gathered[layer]])
        returned = across(expert_out)
        if layer + 1 < sections:
            state, normed, sent = pl.pallas_call(
                step_kernel,
                out_shape=[tok_shape, tok_shape, rows_shape],
                compiler_params=params,
            )(returned, mix_pair, state, gains[layer + 1], pickers[layer + 1])
        else:
            state = pl.pallas_call(
                last_kernel, out_shape=tok_shape, compiler_params=params
            )(returned, mix_pair, state)
        outs.append(state)
    states = lax.all_to_all(jnp.stack(outs), "section", 0, 0, tiled=True)
    return states[None]


def solution(mesh):
    in_specs = (
        P(None, "dp", None),
        P("section", None, "dp", None),
        P("section", None),
        P("section", None, None),
        P("section", "dp", None, None),
        P("section", "dp", None, None),
        P("section", "dp", None, None),
    )
    out_specs = P("section", None, "dp", None)
    return jax.shard_map(
        on_device, mesh=mesh, in_specs=in_specs, out_specs=out_specs, check_vma=False
    )
```

time: 660 us -> 610 us (0.924)
  blocking collectives: 104 us -> 12.7 us
  waiting for transfers between devices: 378 us -> 433 us
  local copies, waits for them, and re-layouts: 35.3 us -> 14.7 us
  Pallas kernels: 23.1 us -> 40.6 us
  matrix products: 12.9 us -> 1.47 us
    all_to_all x9, waiting for transfers between devices: 358 us -> 205 us  [the longest x8 201 us: across(): moved = lax.all_to_all(blocks, 'dp', 0, 0, tiled=True)]
    ppermute x0 -> x7, waiting for transfers between devices: none -> 112 us  [the longest x6 111 us: shifted(): lax.ppermute(part, 'section', [(i, (i + by) % sections) for i in range(se...]
    all_gather x9 -> x4, waiting for transfers between devices: 16.4 us -> 115 us  [the longest x3 89.9 us: on_device(): gathered.append(lax.all_gather(part, 'section', axis=0))]
    all_to_all x2 -> x0, blocking collectives: 91.4 us -> none  [on_device(): arrived = lax.all_to_all(sent, 'dp', 0, 0, tiled=True)]
    reshape x16 -> x2, local copies, waits for them, and re-layouts: 20 us -> 0.16 us  [the longest x1 0.15 us: on_device(): router_half = after(router_half.reshape(-1, LANES), first_part)]
    pallas_call x4 -> x10, Pallas kernels: 23.1 us -> 40.6 us  [the longest x4 28.7 us: expert_mlp(): pl.pallas_call(lambda *refs: mlp_kernel(split, *refs), out_shape=jax.Shap...]
    ppermute x0 -> x7, starting transfers between devices: none -> 12.1 us  [the longest x6 10.6 us: shifted(): lax.ppermute(part, 'section', [(i, (i + by) % sections) for i in range(se...]
    all_to_all x9, starting transfers between devices: 78.4 us -> 66.8 us  [the longest x8 62 us: across(): moved = lax.all_to_all(blocks, 'dp', 0, 0, tiled=True)]
  transfers between devices with their start and end apart: 18 -> 20, of which waited for: 12 -> 19; matrix products, arithmetic and copies ran while one was open for 8% -> 3% of each run, Pallas kernels for 3% -> 4%
where the time goes in v2:
time: 610 us; the launch traced here: 609 us
  waiting for transfers between devices  433 us (71%)
  starting transfers between devices  79 us (13%)
  Pallas kernels  40.6 us (7%)
  local copies, waits for them, and re-layouts  14.7 us (2%)
  between operations  13.8 us (2%)
  other arithmetic  13.6 us (2%)
  blocking collectives  12.7 us (2%)
    all_to_all x8, waiting for transfers between devices, across(): moved = lax.all_to_all(blocks, 'dp', 0, 0, tiled=True)  201 us
    ppermute x6, waiting for transfers between devices, shifted(): lax.ppermute(part, 'section', [(i, (i + by) % sections) for i in range(se...  111 us
    all_gather x3, waiting for transfers between devices, on_device(): gathered.append(lax.all_gather(part, 'section', axis=0))  89.9 us
    all_to_all x8, starting transfers between devices, across(): moved = lax.all_to_all(blocks, 'dp', 0, 0, tiled=True)  62 us
    pallas_call x4, Pallas kernels, expert_mlp(): pl.pallas_call(lambda *refs: mlp_kernel(split, *refs), out_shape=jax.Shap...  28.7 us
    all_gather x1, waiting for transfers between devices, on_device(): gathered = [lax.all_gather(first_part, 'section', axis=0)]  24.8 us
    all_to_all x1, blocking collectives, on_device(): states = lax.all_to_all(jnp.stack(outs), 'section', 0, 0, tiled=True)  12.7 us
  transfers between devices with their start and end apart: 20, of which 19 were waited for; matrix products, arithmetic and copies ran while one was open for 3% of the time, Pallas kernels for 4%

profile of v2, /device:TPU:1, one launch (start us, length us, event | category | flops | bytes accessed | tf_op | source)
XLA Modules:
  0.0 608.6 jit_solution(4409338047665711721)
XLA Ops:
  6.5 7.3 %shard_map.73 = (bf16[768,1536]{1,0:T(8,128)(2,1)S(1)}, bf16[768,1536]{1,0:T(8,128)(2,1)}, bf16[768,1536]{1,0:T(8,128)(2,1)}, bf16[768,1536]{1,0:T(8,128)(2,1)}) custom-call(s32[1]{0:T(128)} %bitcast.1.first_ref, bf16[2048,768]{1,0:T(8,128)(2,1)} %bitcast.136, bf16[2048,768]{1,0:T(8,128)(2,1)} %bitcast.137, bf16[768,2048]{1,0:T(8,128)(2,1)} %bitcast.138), custom_call_target="tpu_custom_call" | custom-call | tf_op jit(solution)/shard_map/pallas_call | solution.py:154
  19.7 47.0 %collective-permute-done = bf16[768,1536]{1,0:T(8,128)(2,1)} collective-permute-done((bf16[768,1536]{1,0:T(8,128)(2,1)}, bf16[768,1536]{1,0:T(8,128)(2,1)}, u32[]{:S(2)}, u32[]{:S(2)}) %collective-permute-start) | collective-permute-done | bytes 2359328 | tf_op jit(solution)/shard_map/ppermute | solution.py:181
  66.7 53.5 %collective-permute-done.1 = bf16[768,1536]{1,0:T(8,128)(2,1)} collective-permute-done((bf16[768,1536]{1,0:T(8,128)(2,1)}, bf16[768,1536]{1,0:T(8,128)(2,1)}, u32[]{:S(2)}, u32[]{:S(2)}) %collective-permute-start.1) | collective-permute-done | bytes 2359328 | tf_op jit(solution)/shard_map/ppermute | solution.py:181
  125.3 4.8 all-to-all-start
  137.7 14.1 %all-to-all-start.1 = ((bf16[64,96,128]{2,1,0:T(8,128)(2,1)}), bf16[64,96,128]{2,1,0:T(8,128)(2,1)}, u32[]{:S(2)}, u32[]{:S(2)}) async-start(bf16[64,96,128]{2,1,0:T(8,128)(2,1)} %bitcast.119), calls=%async_computation.1 | async-start | bytes 3145728 | tf_op jit(solution)/shard_map/all_to_all | solution.py:236
  151.9 39.7 %all-to-all-done.1 = bf16[64,96,128]{2,1,0:T(8,128)(2,1)} async-done(((bf16[64,96,128]{2,1,0:T(8,128)(2,1)}), bf16[64,96,128]{2,1,0:T(8,128)(2,1)}, u32[]{:S(2)}, u32[]{:S(2)}) %all-to-all-start.1) | async-done | bytes 1572896 | tf_op jit(solution)/shard_map/all_to_all | solution.py:236
  191.5 5.2 select_select_fusion
  197.5 24.8 %all-gather.9.cloned.1.call-done = bf16[3072,1536]{1,0:T(8,128)(2,1)} async-done(((bf16[768,1536]{1,0:T(8,128)(2,1)}), bf16[3072,1536]{1,0:T(8,128)(2,1)}) %all-gather.9.cloned.1.call-update) | async-done | bytes 9437200 | tf_op jit(solution)/shard_map/all_gather | solution.py:205
  222.3 9.1 %shard_map.75 = bf16[384,16,128]{2,1,0:T(8,128)(2,1)} custom-call(bf16[384,16,128]{2,1,0:T(8,128)(2,1)} %bitcast.13.refs_0_, bf16[4,768,1536]{2,1,0:T(8,128)(2,1)} %bitcast.133), custom_call_target="tpu_custom_call" | custom-call | tf_op jit(solution)/shard_map/pallas_call | solution.py:105
  231.4 10.8 %all-to-all-start.2 = ((bf16[64,96,128]{2,1,0:T(8,128)(2,1)}), bf16[64,96,128]{2,1,0:T(8,128)(2,1)S(1)}, u32[]{:S(2)}, u32[]{:S(2)}) async-start(bf16[64,96,128]{2,1,0:T(8,128)(2,1)} %bitcast.15), calls=%async_computation.2 | async-start | bytes 3145728 | tf_op jit(solution)/shard_map/all_to_all | solution.py:236
  247.4 4.8 collective-permute-done.3
  252.2 5.5 collective-permute-done.4
  265.6 16.5 %all-to-all-done.2 = bf16[64,96,128]{2,1,0:T(8,128)(2,1)S(1)} async-done(((bf16[64,96,128]{2,1,0:T(8,128)(2,1)}), bf16[64,96,128]{2,1,0:T(8,128)(2,1)S(1)}, u32[]{:S(2)}, u32[]{:S(2)}) %all-to-all-start.2) | async-done | bytes 1572896 | tf_op jit(solution)/shard_map/all_to_all | solution.py:236
  284.4 6.1 %all-to-all-start.3 = ((bf16[64,96,128]{2,1,0:T(8,128)(2,1)}), bf16[64,96,128]{2,1,0:T(8,128)(2,1)S(1)}, u32[]{:S(2)}, u32[]{:S(2)}) async-start(bf16[64,96,128]{2,1,0:T(8,128)(2,1)} %bitcast.120), calls=%async_computation.3 | async-start | bytes 3145728 | tf_op jit(solution)/shard_map/all_to_all | solution.py:236
  291.1 34.2 %all-gather.11.cloned.1.call-done = bf16[3072,1536]{1,0:T(8,128)(2,1)} async-done(((bf16[768,1536]{1,0:T(8,128)(2,1)}), bf16[3072,1536]{1,0:T(8,128)(2,1)}) %all-gather.11.cloned.1.call-update) | async-done | bytes 9437200 | tf_op jit(solution)/shard_map/all_gather | solution.py:258
  325.3 5.0 all-to-all-done.3
  330.3 6.5 %shard_map.77 = bf16[384,16,128]{2,1,0:T(8,128)(2,1)S(1)} custom-call(bf16[384,16,128]{2,1,0:T(8,128)(2,1)S(1)} %bitcast.116, bf16[4,768,1536]{2,1,0:T(8,128)(2,1)} %bitcast.132), custom_call_target="tpu_custom_call" | custom-call | tf_op jit(solution)/shard_map/pallas_call | solution.py:105
  338.0 6.3 %all-to-all-start.4 = ((bf16[64,96,128]{2,1,0:T(8,128)(2,1)}), bf16[64,96,128]{2,1,0:T(8,128)(2,1)S(1)}, u32[]{:S(2)}, u32[]{:S(2)}) async-start(bf16[64,96,128]{2,1,0:T(8,128)(2,1)} %bitcast.114), calls=%async_computation.4 | async-start | bytes 3145728 | tf_op jit(solution)/shard_map/all_to_all | solution.py:236
  345.4 38.7 %all-to-all-done.4 = bf16[64,96,128]{2,1,0:T(8,128)(2,1)S(1)} async-done(((bf16[64,96,128]{2,1,0:T(8,128)(2,1)}), bf16[64,96,128]{2,1,0:T(8,128)(2,1)S(1)}, u32[]{:S(2)}, u32[]{:S(2)}) %all-to-all-start.4) | async-done | bytes 1572896 | tf_op jit(solution)/shard_map/all_to_all | solution.py:236
  386.4 6.1 %all-to-all-start.5 = ((bf16[64,96,128]{2,1,0:T(8,128)(2,1)}), bf16[64,96,128]{2,1,0:T(8,128)(2,1)S(1)}, u32[]{:S(2)}, u32[]{:S(2)}) async-start(bf16[64,96,128]{2,1,0:T(8,128)(2,1)} %bitcast.121), calls=%async_computation.5 | async-start | bytes 3145728 | tf_op jit(solution)/shard_map/all_to_all | solution.py:236
  392.5 30.2 %all-gather.13.cloned.1.call-done = bf16[3072,1536]{1,0:T(8,128)(2,1)} async-done(((bf16[768,1536]{1,0:T(8,128)(2,1)}), bf16[3072,1536]{1,0:T(8,128)(2,1)}) %all-gather.13.cloned.1.call-update) | async-done | bytes 9437200 | tf_op jit(solution)/shard_map/all_gather | solution.py:258
  422.7 9.6 %all-to-all-done.5 = bf16[64,96,128]{2,1,0:T(8,128)(2,1)S(1)} async-done(((bf16[64,96,128]{2,1,0:T(8,128)(2,1)}), bf16[64,96,128]{2,1,0:T(8,128)(2,1)S(1)}, u32[]{:S(2)}, u32[]{:S(2)}) %all-to-all-start.5) | async-done | bytes 1572896 | tf_op jit(solution)/shard_map/all_to_all | solution.py:236
  432.3 6.5 %shard_map.79 = bf16[384,16,128]{2,1,0:T(8,128)(2,1)S(1)} custom-call(bf16[384,16,128]{2,1,0:T(8,128)(2,1)S(1)} %bitcast.117, bf16[4,768,1536]{2,1,0:T(8,128)(2,1)} %bitcast.131), custom_call_target="tpu_custom_call" | custom-call | tf_op jit(solution)/shard_map/pallas_call | solution.py:105
  440.0 6.2 %all-to-all-start.6 = ((bf16[64,96,128]{2,1,0:T(8,128)(2,1)}), bf16[64,96,128]{2,1,0:T(8,128)(2,1)S(1)}, u32[]{:S(2)}, u32[]{:S(2)}) async-start(bf16[64,96,128]{2,1,0:T(8,128)(2,1)} %bitcast.115), calls=%async_computation.6 | async-start | bytes 3145728 | tf_op jit(solution)/shard_map/all_to_all | solution.py:236
  447.3 38.7 %all-to-all-done.6 = bf16[64,96,128]{2,1,0:T(8,128)(2,1)S(1)} async-done(((bf16[64,96,128]{2,1,0:T(8,128)(2,1)}), bf16[64,96,128]{2,1,0:T(8,128)(2,1)S(1)}, u32[]{:S(2)}, u32[]{:S(2)}) %all-to-all-start.6) | async-done | bytes 1572896 | tf_op jit(solution)/shard_map/all_to_all | solution.py:236
  488.4 6.1 %all-to-all-start.7 = ((bf16[64,96,128]{2,1,0:T(8,128)(2,1)}), bf16[64,96,128]{2,1,0:T(8,128)(2,1)S(1)}, u32[]{:S(2)}, u32[]{:S(2)}) async-start(bf16[64,96,128]{2,1,0:T(8,128)(2,1)} %bitcast.122), calls=%async_computation.7 | async-start | bytes 3145728 | tf_op jit(solution)/shard_map/all_to_all | solution.py:236
  494.5 25.5 %all-gather.15.cloned.1.call-done = bf16[3072,1536]{1,0:T(8,128)(2,1)} async-done(((bf16[768,1536]{1,0:T(8,128)(2,1)}), bf16[3072,1536]{1,0:T(8,128)(2,1)}) %all-gather.15.cloned.1.call-update) | async-done | bytes 9437200 | tf_op jit(solution)/shard_map/all_gather | solution.py:258
  520.0 14.3 %all-to-all-done.7 = bf16[64,96,128]{2,1,0:T(8,128)(2,1)S(1)} async-done(((bf16[64,96,128]{2,1,0:T(8,128)(2,1)}), bf16[64,96,128]{2,1,0:T(8,128)(2,1)S(1)}, u32[]{:S(2)}, u32[]{:S(2)}) %all-to-all-start.7) | async-done | bytes 1572896 | tf_op jit(solution)/shard_map/all_to_all | solution.py:236
  534.3 6.5 %shard_map.81 = bf16[384,16,128]{2,1,0:T(8,128)(2,1)S(1)} custom-call(bf16[384,16,128]{2,1,0:T(8,128)(2,1)S(1)} %bitcast.118, bf16[4,768,1536]{2,1,0:T(8,128)(2,1)} %bitcast.134), custom_call_target="tpu_custom_call" | custom-call | tf_op jit(solution)/shard_map/pallas_call | solution.py:105
  542.0 6.3 %all-to-all-start.8 = ((bf16[64,96,128]{2,1,0:T(8,128)(2,1)}), bf16[64,96,128]{2,1,0:T(8,128)(2,1)S(1)}, u32[]{:S(2)}, u32[]{:S(2)}) async-start(bf16[64,96,128]{2,1,0:T(8,128)(2,1)} %bitcast.113), calls=%async_computation.8 | async-start | bytes 3145728 | tf_op jit(solution)/shard_map/all_to_all | solution.py:236
  549.4 38.7 %all-to-all-done.8 = bf16[64,96,128]{2,1,0:T(8,128)(2,1)S(1)} async-done(((bf16[64,96,128]{2,1,0:T(8,128)(2,1)}), bf16[64,96,128]{2,1,0:T(8,128)(2,1)S(1)}, u32[]{:S(2)}, u32[]{:S(2)}) %all-to-all-start.8) | async-done | bytes 1572896 | tf_op jit(solution)/shard_map/all_to_all | solution.py:236
  588.6 12.7 %all_to_all.50 = bf16[4,32,2048]{2,1,0:T(8,128)(2,1)S(1)} all-to-all(bf16[4,32,2048]{2,1,0:T(8,128)(2,1)S(1)} %pad_maximum_fusion.1), channel_id=1, replica_groups=mesh['section'=4,'dp'=64] {'section'}, dimensions={0} | all-to-all | bytes 1048576 | tf_op jit(solution)/shard_map/all_to_all | solution.py:272
  (146 shorter events, 47.7 us)
Async XLA Ops:
  6.5 123.6 %copy-start = (bf16[4,32,2048]{2,1,0:T(8,128)(2,1)S(1)}, bf16[4,32,2048]{2,1,0:T(8,128)(2,1)}, u32[]{:S(2)}) copy-start(bf16[4,32,2048]{2,1,0:T(8,128)(2,1)} %param.7) | copy-start | bytes 1572868
  6.5 215.8 %all-gather.9.cloned.1.call-start = ((), (), s32[]{:S(2)}) async-start(), calls=%async_computation.10 | async-start | bytes 11796480 | tf_op jit(solution)/shard_map/all_gather | solution.py:205
  13.8 52.8 %collective-permute-start = (bf16[768,1536]{1,0:T(8,128)(2,1)}, bf16[768,1536]{1,0:T(8,128)(2,1)}, u32[]{:S(2)}, u32[]{:S(2)}) collective-permute-start(bf16[768,1536]{1,0:T(8,128)(2,1)} %get-tuple-element.27), channel_id=1, source_target_pairs={{0,64},{64,128},{128,192},{192,0},{1,65},{65,129},{129,193},{193,1... | collective-permute-start | bytes 7077896 | tf_op jit(solution)/shard_map/ppermute | solution.py:181
  16.0 104.1 %collective-permute-start.1 = (bf16[768,1536]{1,0:T(8,128)(2,1)}, bf16[768,1536]{1,0:T(8,128)(2,1)}, u32[]{:S(2)}, u32[]{:S(2)}) collective-permute-start(bf16[768,1536]{1,0:T(8,128)(2,1)} %get-tuple-element.28), channel_id=1, source_target_pairs={{0,128},{64,192},{128,0},{192,64},{1,129},{65,193},{129,1},{193,65... | collective-permute-start | bytes 7077896 | tf_op jit(solution)/shard_map/ppermute | solution.py:181
  18.6 101.5 %collective-permute-start.2 = (bf16[768,1536]{1,0:T(8,128)(2,1)}, bf16[768,1536]{1,0:T(8,128)(2,1)}, u32[]{:S(2)}, u32[]{:S(2)}) collective-permute-start(bf16[768,1536]{1,0:T(8,128)(2,1)} %get-tuple-element.29), channel_id=1, source_target_pairs={{0,192},{64,0},{128,64},{192,128},{1,193},{65,1},{129,65},{193,129... | collective-permute-start | bytes 7077896 | tf_op jit(solution)/shard_map/ppermute | solution.py:181
  125.3 9.1 %all-to-all-start = ((bf16[4,18,128]{2,1,0:T(8,128)(2,1)}), bf16[4,18,128]{2,1,0:T(8,128)(2,1)S(1)}, u32[]{:S(2)}, u32[]{:S(2)}) async-start(bf16[4,18,128]{2,1,0:T(8,128)(2,1)} %pad_maximum_fusion.7), calls=%async_computation | async-start | bytes 49152 | tf_op jit(solution)/shard_map/all_to_all | solution.py:193
  136.5 1.2 copy-start.5
  137.7 53.8 %all-to-all-start.1 = ((bf16[64,96,128]{2,1,0:T(8,128)(2,1)}), bf16[64,96,128]{2,1,0:T(8,128)(2,1)}, u32[]{:S(2)}, u32[]{:S(2)}) async-start(bf16[64,96,128]{2,1,0:T(8,128)(2,1)} %bitcast.119), calls=%async_computation.1 | async-start | bytes 3145728 | tf_op jit(solution)/shard_map/all_to_all | solution.py:236
  151.8 173.5 %all-gather.11.cloned.1.call-start = ((), (), s32[]{:S(2)}) async-start(), calls=%async_computation.11 | async-start | bytes 11796480 | tf_op jit(solution)/shard_map/all_gather | solution.py:258
  196.8 225.9 %all-gather.13.cloned.1.call-start = ((), (), s32[]{:S(2)}) async-start(), calls=%async_computation.12 | async-start | bytes 11796480 | tf_op jit(solution)/shard_map/all_gather | solution.py:258
  231.4 10.8 %copy-start.15 = (bf16[1,2048,64]{1,2,0:T(8,128)(2,1)S(1)}, bf16[1,2048,64]{1,2,0:T(8,128)(2,1)}, u32[]{:S(2)}) copy-start(bf16[1,2048,64]{1,2,0:T(8,128)(2,1)} %param.10) | copy-start | bytes 786436
  231.4 50.6 %all-to-all-start.2 = ((bf16[64,96,128]{2,1,0:T(8,128)(2,1)}), bf16[64,96,128]{2,1,0:T(8,128)(2,1)S(1)}, u32[]{:S(2)}, u32[]{:S(2)}) async-start(bf16[64,96,128]{2,1,0:T(8,128)(2,1)} %bitcast.15), calls=%async_computation.2 | async-start | bytes 3145728 | tf_op jit(solution)/shard_map/all_to_all | solution.py:236
  242.6 9.6 %collective-permute-start.3 = (bf16[512,128]{1,0:T(8,128)(2,1)S(1)}, bf16[512,128]{1,0:T(8,128)(2,1)S(1)}, u32[]{:S(2)}, u32[]{:S(2)}) collective-permute-start(bf16[512,128]{1,0:T(8,128)(2,1)S(1)} %reshape.143), channel_id=1, source_target_pairs={{0,64},{64,128},{128,192},{192,0},{1,65},{65,129},{129,193},{193,1... | collective-permute-start | bytes 393224 | tf_op jit(solution)/shard_map/ppermute | solution.py:181
  244.1 13.6 %collective-permute-start.4 = (bf16[512,128]{1,0:T(8,128)(2,1)S(1)}, bf16[512,128]{1,0:T(8,128)(2,1)S(1)}, u32[]{:S(2)}, u32[]{:S(2)}) collective-permute-start(bf16[512,128]{1,0:T(8,128)(2,1)S(1)} %reshape.143), channel_id=1, source_target_pairs={{0,128},{64,192},{128,0},{192,64},{1,129},{65,193},{129,1},{193,65... | collective-permute-start | bytes 393224 | tf_op jit(solution)/shard_map/ppermute | solution.py:181
  245.5 12.8 %collective-permute-start.5 = (bf16[512,128]{1,0:T(8,128)(2,1)S(1)}, bf16[512,128]{1,0:T(8,128)(2,1)S(1)}, u32[]{:S(2)}, u32[]{:S(2)}) collective-permute-start(bf16[512,128]{1,0:T(8,128)(2,1)S(1)} %reshape.143), channel_id=1, source_target_pairs={{0,192},{64,0},{128,64},{192,128},{1,193},{65,1},{129,65},{193,129... | collective-permute-start | bytes 393224 | tf_op jit(solution)/shard_map/ppermute | solution.py:181
  259.2 3.4 collective-permute-start.6
  283.2 1.2 copy-start.6
  284.4 45.9 %all-to-all-start.3 = ((bf16[64,96,128]{2,1,0:T(8,128)(2,1)}), bf16[64,96,128]{2,1,0:T(8,128)(2,1)S(1)}, u32[]{:S(2)}, u32[]{:S(2)}) async-start(bf16[64,96,128]{2,1,0:T(8,128)(2,1)} %bitcast.120), calls=%async_computation.3 | async-start | bytes 3145728 | tf_op jit(solution)/shard_map/all_to_all | solution.py:236
  290.5 229.5 %all-gather.15.cloned.1.call-start = ((), (), s32[]{:S(2)}) async-start(), calls=%async_computation.13 | async-start | bytes 11796480 | tf_op jit(solution)/shard_map/all_gather | solution.py:258
  338.0 6.3 %copy-start.14 = (f32[1,32,64,6]{1,3,2,0:T(8,128)S(1)}, f32[1,32,64,6]{1,3,2,0:T(8,128)}, u32[]{:S(2)}) copy-start(f32[1,32,64,6]{1,3,2,0:T(8,128)} %get-tuple-element.52) | copy-start | bytes 147460
  338.0 6.4 %copy-start.11 = (bf16[1,1024,128]{2,1,0:T(8,128)(2,1)S(1)}, bf16[1,1024,128]{2,1,0:T(8,128)(2,1)}, u32[]{:S(2)}) copy-start(bf16[1,1024,128]{2,1,0:T(8,128)(2,1)} %get-tuple-element.56) | copy-start | bytes 786436
  338.0 46.1 %all-to-all-start.4 = ((bf16[64,96,128]{2,1,0:T(8,128)(2,1)}), bf16[64,96,128]{2,1,0:T(8,128)(2,1)S(1)}, u32[]{:S(2)}, u32[]{:S(2)}) async-start(bf16[64,96,128]{2,1,0:T(8,128)(2,1)} %bitcast.114), calls=%async_computation.4 | async-start | bytes 3145728 | tf_op jit(solution)/shard_map/all_to_all | solution.py:236
  386.4 45.9 %all-to-all-start.5 = ((bf16[64,96,128]{2,1,0:T(8,128)(2,1)}), bf16[64,96,128]{2,1,0:T(8,128)(2,1)S(1)}, u32[]{:S(2)}, u32[]{:S(2)}) async-start(bf16[64,96,128]{2,1,0:T(8,128)(2,1)} %bitcast.121), calls=%async_computation.5 | async-start | bytes 3145728 | tf_op jit(solution)/shard_map/all_to_all | solution.py:236
  440.0 6.3 %copy-start.13 = (f32[1,32,64,6]{1,3,2,0:T(8,128)S(1)}, f32[1,32,64,6]{1,3,2,0:T(8,128)}, u32[]{:S(2)}) copy-start(f32[1,32,64,6]{1,3,2,0:T(8,128)} %get-tuple-element.51) | copy-start | bytes 147460
  440.0 6.4 %copy-start.10 = (bf16[1,1024,128]{2,1,0:T(8,128)(2,1)S(1)}, bf16[1,1024,128]{2,1,0:T(8,128)(2,1)}, u32[]{:S(2)}) copy-start(bf16[1,1024,128]{2,1,0:T(8,128)(2,1)} %get-tuple-element.57) | copy-start | bytes 786436
  440.0 46.1 %all-to-all-start.6 = ((bf16[64,96,128]{2,1,0:T(8,128)(2,1)}), bf16[64,96,128]{2,1,0:T(8,128)(2,1)S(1)}, u32[]{:S(2)}, u32[]{:S(2)}) async-start(bf16[64,96,128]{2,1,0:T(8,128)(2,1)} %bitcast.115), calls=%async_computation.6 | async-start | bytes 3145728 | tf_op jit(solution)/shard_map/all_to_all | solution.py:236
  487.2 1.2 copy-start.8
  488.4 45.9 %all-to-all-start.7 = ((bf16[64,96,128]{2,1,0:T(8,128)(2,1)}), bf16[64,96,128]{2,1,0:T(8,128)(2,1)S(1)}, u32[]{:S(2)}, u32[]{:S(2)}) async-start(bf16[64,96,128]{2,1,0:T(8,128)(2,1)} %bitcast.122), calls=%async_computation.7 | async-start | bytes 3145728 | tf_op jit(solution)/shard_map/all_to_all | solution.py:236
  542.0 6.3 %copy-start.12 = (f32[1,32,64,6]{1,3,2,0:T(8,128)S(1)}, f32[1,32,64,6]{1,3,2,0:T(8,128)}, u32[]{:S(2)}) copy-start(f32[1,32,64,6]{1,3,2,0:T(8,128)} %get-tuple-element.50) | copy-start | bytes 147460
  542.0 6.4 %copy-start.9 = (bf16[1,1024,128]{2,1,0:T(8,128)(2,1)S(1)}, bf16[1,1024,128]{2,1,0:T(8,128)(2,1)}, u32[]{:S(2)}) copy-start(bf16[1,1024,128]{2,1,0:T(8,128)(2,1)} %get-tuple-element.54) | copy-start | bytes 786436
  542.0 46.1 %all-to-all-start.8 = ((bf16[64,96,128]{2,1,0:T(8,128)(2,1)}), bf16[64,96,128]{2,1,0:T(8,128)(2,1)S(1)}, u32[]{:S(2)}, u32[]{:S(2)}) async-start(bf16[64,96,128]{2,1,0:T(8,128)(2,1)} %bitcast.113), calls=%async_computation.8 | async-start | bytes 3145728 | tf_op jit(solution)/shard_map/all_to_all | solution.py:236
  588.0 14.1 %copy-start.1 = (bf16[4,32,2048]{2,1,0:T(8,128)(2,1)S(1)}, bf16[4,32,2048]{2,1,0:T(8,128)(2,1)}, u32[]{:S(2)}) copy-start(bf16[4,32,2048]{2,1,0:T(8,128)(2,1)} %param.7) | copy-start | bytes 1572868
  (6 other events, 6.3 us)
Sparse Core Ops, SparseCore 0:
  123.8 98.4 all-gather.8
  224.1 101.1 all-gather.10
  327.1 95.5 all-gather.12
  424.4 95.5 all-gather.14

commit v3 on v2

--- a/solution.py
+++ b/solution.py
@@ -13,6 +13,20 @@
 def normalise(wide, gain_row):
     inv_rms = lax.rsqrt(jnp.mean(wide * wide, axis=1, keepdims=True) + EPS)
     return (wide * inv_rms * gain_row).astype(jnp.bfloat16)
+
+
+def send_rows(rows, out_ref, out_buf, sems):
+    half = out_buf.shape[0] // 2
+    sends = []
+    for block in range(2):
+        span = pl.ds(block * half, half)
+        part = rows[block * half : (block + 1) * half].astype(jnp.bfloat16)
+        out_buf[span] = part.reshape(half, *out_buf.shape[1:])
+        send = pltpu.make_async_copy(out_buf.at[span], out_ref.at[span], sems.at[block])
+        send.start()
+        sends.append(send)
+    for send in sends:
+        send.wait()
 
 
 def pack_rows(picker, normed, sent_ref):
@@ -49,8 +63,8 @@
 
 
 def mlp_kernel(split, x_ref, *refs):
-    sources = refs[:-4]
-    out_ref, held, act, sems = refs[-4:]
+    sources = refs[:-6]
+    out_ref, held, act, out_buf, sems, out_sems = refs[-6:]
     count, depth, both = held.shape
     ff = both // 2
     top = x_ref.shape[1] * x_ref.shape[2] // count
@@ -95,7 +109,7 @@
             )
             total = term if total is None else total + term
         outs.append(total.astype(jnp.bfloat16))
-    out_ref[...] = jnp.concatenate(outs, axis=1).reshape(out_ref.shape)
+    send_rows(jnp.concatenate(outs, axis=1), out_ref, out_buf, out_sems)
 
 
 def expert_mlp(rows, sources):
@@ -107,11 +121,13 @@
         out_shape=jax.ShapeDtypeStruct(rows.shape, jnp.bfloat16),
         in_specs=[pl.BlockSpec(memory_space=pltpu.VMEM)]
         + [pl.BlockSpec(memory_space=pl.ANY)] * len(sources),
-        out_specs=pl.BlockSpec(memory_space=pltpu.VMEM),
+        out_specs=pl.BlockSpec(memory_space=pltpu.HBM),
         scratch_shapes=[
             pltpu.VMEM((count, depth, both), jnp.bfloat16),
             pltpu.VMEM((rows.shape[0], both), jnp.float32),
+            pltpu.VMEM(rows.shape, jnp.bfloat16),
             pltpu.SemaphoreType.DMA((2, count)),
+            pltpu.SemaphoreType.DMA((2,)),
         ],
         compiler_params=pltpu.CompilerParams(vmem_limit_bytes=VMEM_LIMIT),
     )(rows, *sources)
@@ -157,6 +173,36 @@
         out_shape=[out] * count,
         compiler_params=pltpu.CompilerParams(vmem_limit_bytes=VMEM_LIMIT),
     )(first.reshape(1).astype(jnp.int32), gate, up, down)
+
+
+def pick_kernel(which_ref, *refs):
+    sources, (out_ref, buf, sems) = refs[:-3], refs[-3:]
+    for place, source in enumerate(sources):
+
+        @pl.when(which_ref[0] == place)
+        def _(source=source):
+            fetch = pltpu.make_async_copy(source, buf, sems.at[0])
+            fetch.start()
+            fetch.wait()
+
+    send = pltpu.make_async_copy(buf, out_ref, sems.at[1])
+    send.start()
+    send.wait()
+
+
+def pick_one(which, arrays):
+    return pl.pallas_call(
+        pick_kernel,
+        out_shape=jax.ShapeDtypeStruct(arrays[0].shape, arrays[0].dtype),
+        in_specs=[pl.BlockSpec(memory_space=pltpu.SMEM)]
+        + [pl.BlockSpec(memory_space=pl.ANY)] * len(arrays),
+        out_specs=pl.BlockSpec(memory_space=pltpu.HBM),
+        scratch_shapes=[
+            pltpu.VMEM(arrays[0].shape, arrays[0].dtype),
+            pltpu.SemaphoreType.DMA((2,)),
+        ],
+        compiler_params=pltpu.CompilerParams(vmem_limit_bytes=VMEM_LIMIT),
+    )(which.reshape(1).astype(jnp.int32), *arrays)
 
 
 def after(values, *tokens):
@@ -201,7 +247,7 @@
     def own_part(layer, held):
         return lax.select_n(lax.rem(section + sections - layer, sections), *held)
 
-    first_part = own_part(0, parts)
+    first_part = pick_one(section, parts)
     gathered = [lax.all_gather(first_part, "section", axis=0)]
 
     dp_count = lax.axis_size("dp")
@@ -239,7 +285,9 @@
     state = lax.dynamic_index_in_dim(inputs, section, 0, keepdims=False)
     state = after(state, first_part)
     normed, sent = pl.pallas_call(
-        first_kernel, out_shape=[tok_shape, rows_shape], compiler_params=params
+        first_kernel,
+        out_shape=[tok_shape, rows_shape],
+        compiler_params=params,
     )(state, gains[0], pickers[0])
     outs = []
     for layer in range(sections):
@@ -257,6 +305,12 @@
                 part = own_part(later, held)
                 gathered.append(lax.all_gather(part, "section", axis=0))
         expert_out = expert_mlp(arrived, [gathered[layer]])
+        if layer + 1 == sections:
+            moved = []
+            for by in range(1, sections):
+                pick = jnp.minimum(lax.rem(section + by, sections), sections - 2)
+                moved.append(shifted(lax.select_n(pick, *outs), by))
+            expert_out, moved = lax.optimization_barrier((expert_out, moved))
         returned = across(expert_out)
         if layer + 1 < sections:
             state, normed, sent = pl.pallas_call(
@@ -269,8 +323,17 @@
                 last_kernel, out_shape=tok_shape, compiler_params=params
             )(returned, mix_pair, state)
         outs.append(state)
-    states = lax.all_to_all(jnp.stack(outs), "section", 0, 0, tiled=True)
-    return states[None]
+    last = sections - 1
+    mine = lax.select_n(section, *outs)
+    states = []
+    for micro in range(micro_count):
+        apart = lax.rem(section + sections - micro, sections)
+        home = lax.select_n(apart, mine, *moved)
+        if micro != last:
+            final = lax.ppermute(outs[last], "section", [(micro, last)])
+            home = jnp.where(section == last, final, home)
+        states.append(home)
+    return jnp.stack(states)[None]
 
 
 def solution(mesh):

time: 610 us -> 620 us (1.016)
  starting transfers between devices: 79 us -> 98.8 us
  blocking collectives: 12.7 us -> 0 us
    all_gather x3, waiting for transfers between devices: 89.9 us -> 71.6 us  [on_device(): gathered.append(lax.all_gather(part, 'section', axis=0))]
    all_to_all x8, waiting for transfers between devices: 201 us -> 214 us  [across(): moved = lax.all_to_all(blocks, 'dp', 0, 0, tiled=True)]
    all_to_all x1 -> x0, blocking collectives: 12.7 us -> none  [on_device(): states = lax.all_to_all(jnp.stack(outs), 'section', 0, 0, tiled=True)]
    all_to_all x8, starting transfers between devices: 62 us -> 72.2 us  [across(): moved = lax.all_to_all(blocks, 'dp', 0, 0, tiled=True)]
    ppermute x6 -> x9, starting transfers between devices: 10.6 us -> 15.2 us  [shifted(): lax.ppermute(part, 'section', [(i, (i + by) % sections) for i in range(se...]
    ppermute x6 -> x9, waiting for transfers between devices: 111 us -> 111 us  [shifted(): lax.ppermute(part, 'section', [(i, (i + by) % sections) for i in range(se...]
  transfers between devices with their start and end apart: 20 -> 26, of which waited for: 19 -> 20; matrix products, arithmetic and copies ran while one was open for 3% -> 3% of each run, Pallas kernels for 4% -> 6%
where the time goes in v3:
time: 620 us; the launch traced here: 614 us
  waiting for transfers between devices  431 us (70%)
  starting transfers between devices  98.8 us (16%)
  Pallas kernels  43.9 us (7%)
  between operations  14.2 us (2%)
  local copies, waits for them, and re-layouts  12.5 us (2%)
  other arithmetic  11.8 us (2%)
    all_to_all x8, waiting for transfers between devices, across(): moved = lax.all_to_all(blocks, 'dp', 0, 0, tiled=True)  214 us
    ppermute x9, waiting for transfers between devices, shifted(): lax.ppermute(part, 'section', [(i, (i + by) % sections) for i in range(se...  111 us
    all_to_all x8, starting transfers between devices, across(): moved = lax.all_to_all(blocks, 'dp', 0, 0, tiled=True)  72.2 us
    all_gather x3, waiting for transfers between devices, on_device(): gathered.append(lax.all_gather(part, 'section', axis=0))  71.6 us
    pallas_call x4, Pallas kernels, expert_mlp(): pl.pallas_call(lambda *refs: mlp_kernel(split, *refs), out_shape=jax.Shap...  31.1 us
    all_gather x1, waiting for transfers between devices, on_device(): gathered = [lax.all_gather(first_part, 'section', axis=0)]  24.7 us
    ppermute x9, starting transfers between devices, shifted(): lax.ppermute(part, 'section', [(i, (i + by) % sections) for i in range(se...  15.2 us
  transfers between devices with their start and end apart: 26, of which 20 were waited for; matrix products, arithmetic and copies ran while one was open for 3% of the time, Pallas kernels for 6%

profile of v3, /device:TPU:1, one launch (start us, length us, event | category | flops | bytes accessed | tf_op | source)
XLA Modules:
  0.0 613.6 jit_solution(12803207274650351796)
XLA Ops:
  6.5 6.6 %shard_map.73 = (bf16[768,1536]{1,0:T(8,128)(2,1)S(1)}, bf16[768,1536]{1,0:T(8,128)(2,1)S(1)}, bf16[768,1536]{1,0:T(8,128)(2,1)}, bf16[768,1536]{1,0:T(8,128)(2,1)}) custom-call(s32[1]{0:T(128)} %bitcast.1.first_ref.which_ref, bf16[2048,768]{1,0:T(8,128)(2,1)} %bitcast.134, bf16[2048,768]{1,0:T(8,128)(2,1)} %bitcast.135, bf16[768,2048]{1,0:T(8,128)(2,1)} %bitcast.136), custom_call_target="tpu_custom_call" | custom-call | tf_op jit(solution)/shard_map/pallas_call | solution.py:170
  18.9 46.7 %collective-permute-done.refs_1_ = bf16[768,1536]{1,0:T(8,128)(2,1)S(1)} collective-permute-done((bf16[768,1536]{1,0:T(8,128)(2,1)S(1)}, bf16[768,1536]{1,0:T(8,128)(2,1)S(1)}, u32[]{:S(2)}, u32[]{:S(2)}) %collective-permute-start) | collective-permute-done | bytes 2359328 | tf_op jit(solution)/shard_map/ppermute | solution.py:227
  65.6 53.5 %collective-permute-done.1.refs_2_ = bf16[768,1536]{1,0:T(8,128)(2,1)S(1)} collective-permute-done((bf16[768,1536]{1,0:T(8,128)(2,1)}, bf16[768,1536]{1,0:T(8,128)(2,1)S(1)}, u32[]{:S(2)}, u32[]{:S(2)}) %collective-permute-start.1) | collective-permute-done | bytes 2359328 | tf_op jit(solution)/shard_map/ppermute | solution.py:227
  124.5 5.1 all-to-all-start
  129.7 4.1 all-to-all-done
  137.2 14.1 %all-to-all-start.1 = ((bf16[64,96,128]{2,1,0:T(8,128)(2,1)}), bf16[64,96,128]{2,1,0:T(8,128)(2,1)}, u32[]{:S(2)}, u32[]{:S(2)}) async-start(bf16[64,96,128]{2,1,0:T(8,128)(2,1)} %bitcast.121), calls=%async_computation.1 | async-start | bytes 3145728 | tf_op jit(solution)/shard_map/all_to_all | solution.py:282
  151.3 39.7 %all-to-all-done.1 = bf16[64,96,128]{2,1,0:T(8,128)(2,1)} async-done(((bf16[64,96,128]{2,1,0:T(8,128)(2,1)}), bf16[64,96,128]{2,1,0:T(8,128)(2,1)}, u32[]{:S(2)}, u32[]{:S(2)}) %all-to-all-start.1) | async-done | bytes 1572896 | tf_op jit(solution)/shard_map/all_to_all | solution.py:282
  191.0 5.3 select_select_fusion
  197.0 24.7 %all-gather.9.cloned.1.call-done = bf16[3072,1536]{1,0:T(8,128)(2,1)} async-done(((bf16[768,1536]{1,0:T(8,128)(2,1)}), bf16[3072,1536]{1,0:T(8,128)(2,1)}) %all-gather.9.cloned.1.call-update) | async-done | bytes 9437200 | tf_op jit(solution)/shard_map/all_gather | solution.py:251
  221.8 8.8 %shard_map.76 = bf16[384,16,128]{2,1,0:T(8,128)(2,1)} custom-call(bf16[384,16,128]{2,1,0:T(8,128)(2,1)} %bitcast.13.refs_0_, bf16[4,768,1536]{2,1,0:T(8,128)(2,1)} %bitcast.132), custom_call_target="tpu_custom_call" | custom-call | tf_op jit(solution)/shard_map/pallas_call | solution.py:119
  230.6 10.8 %all-to-all-start.2 = ((bf16[64,96,128]{2,1,0:T(8,128)(2,1)}), bf16[64,96,128]{2,1,0:T(8,128)(2,1)S(1)}, u32[]{:S(2)}, u32[]{:S(2)}) async-start(bf16[64,96,128]{2,1,0:T(8,128)(2,1)} %bitcast.15), calls=%async_computation.2 | async-start | bytes 3145728 | tf_op jit(solution)/shard_map/all_to_all | solution.py:282
  246.6 4.6 collective-permute-done.3
  251.2 5.5 collective-permute-done.4
  264.8 16.4 %all-to-all-done.2 = bf16[64,96,128]{2,1,0:T(8,128)(2,1)S(1)} async-done(((bf16[64,96,128]{2,1,0:T(8,128)(2,1)}), bf16[64,96,128]{2,1,0:T(8,128)(2,1)S(1)}, u32[]{:S(2)}, u32[]{:S(2)}) %all-to-all-start.2) | async-done | bytes 1572896 | tf_op jit(solution)/shard_map/all_to_all | solution.py:282
  283.6 6.1 all-to-all-start.3
  290.3 34.5 %all-gather.11.cloned.1.call-done = bf16[3072,1536]{1,0:T(8,128)(2,1)} async-done(((bf16[768,1536]{1,0:T(8,128)(2,1)}), bf16[3072,1536]{1,0:T(8,128)(2,1)}) %all-gather.11.cloned.1.call-update) | async-done | bytes 9437200 | tf_op jit(solution)/shard_map/all_gather | solution.py:306
  324.8 4.7 all-to-all-done.3
  329.5 7.4 %shard_map.78 = bf16[384,16,128]{2,1,0:T(8,128)(2,1)} custom-call(bf16[384,16,128]{2,1,0:T(8,128)(2,1)S(1)} %bitcast.119, bf16[4,768,1536]{2,1,0:T(8,128)(2,1)} %bitcast.130), custom_call_target="tpu_custom_call" | custom-call | tf_op jit(solution)/shard_map/pallas_call | solution.py:119
  336.9 6.3 %all-to-all-start.4 = ((bf16[64,96,128]{2,1,0:T(8,128)(2,1)}), bf16[64,96,128]{2,1,0:T(8,128)(2,1)S(1)}, u32[]{:S(2)}, u32[]{:S(2)}) async-start(bf16[64,96,128]{2,1,0:T(8,128)(2,1)} %bitcast.27), calls=%async_computation.4 | async-start | bytes 3145728 | tf_op jit(solution)/shard_map/all_to_all | solution.py:282
  344.3 38.7 %all-to-all-done.4 = bf16[64,96,128]{2,1,0:T(8,128)(2,1)S(1)} async-done(((bf16[64,96,128]{2,1,0:T(8,128)(2,1)}), bf16[64,96,128]{2,1,0:T(8,128)(2,1)S(1)}, u32[]{:S(2)}, u32[]{:S(2)}) %all-to-all-start.4) | async-done | bytes 1572896 | tf_op jit(solution)/shard_map/all_to_all | solution.py:282
  385.3 16.1 %all-to-all-start.5 = ((bf16[64,96,128]{2,1,0:T(8,128)(2,1)}), bf16[64,96,128]{2,1,0:T(8,128)(2,1)S(1)}, u32[]{:S(2)}, u32[]{:S(2)}) async-start(bf16[64,96,128]{2,1,0:T(8,128)(2,1)} %bitcast.124), calls=%async_computation.5 | async-start | bytes 3145728 | tf_op jit(solution)/shard_map/all_to_all | solution.py:282
  401.4 20.7 %all-gather.13.cloned.1.call-done = bf16[3072,1536]{1,0:T(8,128)(2,1)} async-done(((bf16[768,1536]{1,0:T(8,128)(2,1)}), bf16[3072,1536]{1,0:T(8,128)(2,1)}) %all-gather.13.cloned.1.call-update) | async-done | bytes 9437200 | tf_op jit(solution)/shard_map/all_gather | solution.py:306
  422.2 18.9 %all-to-all-done.5 = bf16[64,96,128]{2,1,0:T(8,128)(2,1)S(1)} async-done(((bf16[64,96,128]{2,1,0:T(8,128)(2,1)}), bf16[64,96,128]{2,1,0:T(8,128)(2,1)S(1)}, u32[]{:S(2)}, u32[]{:S(2)}) %all-to-all-start.5) | async-done | bytes 1572896 | tf_op jit(solution)/shard_map/all_to_all | solution.py:282
  441.1 7.5 %shard_map.80 = bf16[384,16,128]{2,1,0:T(8,128)(2,1)} custom-call(bf16[384,16,128]{2,1,0:T(8,128)(2,1)S(1)} %bitcast.120, bf16[4,768,1536]{2,1,0:T(8,128)(2,1)} %bitcast.129), custom_call_target="tpu_custom_call" | custom-call | tf_op jit(solution)/shard_map/pallas_call | solution.py:119
  448.6 6.4 %all-to-all-start.6 = ((bf16[64,96,128]{2,1,0:T(8,128)(2,1)}), bf16[64,96,128]{2,1,0:T(8,128)(2,1)S(1)}, u32[]{:S(2)}, u32[]{:S(2)}) async-start(bf16[64,96,128]{2,1,0:T(8,128)(2,1)} %bitcast.35), calls=%async_computation.6 | async-start | bytes 3145728 | tf_op jit(solution)/shard_map/all_to_all | solution.py:282
  456.2 38.7 %all-to-all-done.6 = bf16[64,96,128]{2,1,0:T(8,128)(2,1)S(1)} async-done(((bf16[64,96,128]{2,1,0:T(8,128)(2,1)}), bf16[64,96,128]{2,1,0:T(8,128)(2,1)S(1)}, u32[]{:S(2)}, u32[]{:S(2)}) %all-to-all-start.6) | async-done | bytes 1572896 | tf_op jit(solution)/shard_map/all_to_all | solution.py:282
  497.2 6.1 all-to-all-start.7
  508.6 16.4 %all-gather.15.cloned.1.call-done = bf16[3072,1536]{1,0:T(8,128)(2,1)} async-done(((bf16[768,1536]{1,0:T(8,128)(2,1)}), bf16[3072,1536]{1,0:T(8,128)(2,1)}) %all-gather.15.cloned.1.call-update) | async-done | bytes 9437200 | tf_op jit(solution)/shard_map/all_gather | solution.py:306
  525.0 18.1 %all-to-all-done.7 = bf16[64,96,128]{2,1,0:T(8,128)(2,1)S(1)} async-done(((bf16[64,96,128]{2,1,0:T(8,128)(2,1)}), bf16[64,96,128]{2,1,0:T(8,128)(2,1)S(1)}, u32[]{:S(2)}, u32[]{:S(2)}) %all-to-all-start.7) | async-done | bytes 1572896 | tf_op jit(solution)/shard_map/all_to_all | solution.py:282
  543.1 7.4 %shard_map.82 = bf16[384,16,128]{2,1,0:T(8,128)(2,1)} custom-call(bf16[384,16,128]{2,1,0:T(8,128)(2,1)S(1)} %bitcast.115, bf16[4,768,1536]{2,1,0:T(8,128)(2,1)} %bitcast.131), custom_call_target="tpu_custom_call" | custom-call | tf_op jit(solution)/shard_map/pallas_call | solution.py:119
  550.6 6.3 %all-to-all-start.8 = ((bf16[64,96,128]{2,1,0:T(8,128)(2,1)}), bf16[64,96,128]{2,1,0:T(8,128)(2,1)S(1)}, u32[]{:S(2)}, u32[]{:S(2)}) async-start(bf16[64,96,128]{2,1,0:T(8,128)(2,1)} %bitcast.43), calls=%async_computation.8 | async-start | bytes 3145728 | tf_op jit(solution)/shard_map/all_to_all | solution.py:282
  557.9 38.7 %all-to-all-done.8 = bf16[64,96,128]{2,1,0:T(8,128)(2,1)S(1)} async-done(((bf16[64,96,128]{2,1,0:T(8,128)(2,1)}), bf16[64,96,128]{2,1,0:T(8,128)(2,1)S(1)}, u32[]{:S(2)}, u32[]{:S(2)}) %all-to-all-start.8) | async-done | bytes 1572896 | tf_op jit(solution)/shard_map/all_to_all | solution.py:282
  (163 shorter events, 54.8 us)
Async XLA Ops:
  6.5 123.0 %copy-start = (bf16[4,32,2048]{2,1,0:T(8,128)(2,1)S(1)}, bf16[4,32,2048]{2,1,0:T(8,128)(2,1)}, u32[]{:S(2)}) copy-start(bf16[4,32,2048]{2,1,0:T(8,128)(2,1)} %param.7) | copy-start | bytes 1572868
  6.5 215.2 %all-gather.9.cloned.1.call-start = ((), (), s32[]{:S(2)}) async-start(), calls=%async_computation.9 | async-start | bytes 11796480 | tf_op jit(solution)/shard_map/all_gather | solution.py:251
  13.1 52.5 %collective-permute-start = (bf16[768,1536]{1,0:T(8,128)(2,1)S(1)}, bf16[768,1536]{1,0:T(8,128)(2,1)S(1)}, u32[]{:S(2)}, u32[]{:S(2)}) collective-permute-start(bf16[768,1536]{1,0:T(8,128)(2,1)S(1)} %get-tuple-element.31), channel_id=1, source_target_pairs={{0,64},{64,128},{128,192},{192,0},{1,65},{65,129},{129,193},{193,1... | collective-permute-start | bytes 7077896 | tf_op jit(solution)/shard_map/ppermute | solution.py:227
  15.2 103.8 %collective-permute-start.1 = (bf16[768,1536]{1,0:T(8,128)(2,1)}, bf16[768,1536]{1,0:T(8,128)(2,1)S(1)}, u32[]{:S(2)}, u32[]{:S(2)}) collective-permute-start(bf16[768,1536]{1,0:T(8,128)(2,1)} %get-tuple-element.32), channel_id=1, source_target_pairs={{0,128},{64,192},{128,0},{192,64},{1,129},{65,193},{129,1},{193,65... | collective-permute-start | bytes 7077896 | tf_op jit(solution)/shard_map/ppermute | solution.py:227
  17.9 101.2 %collective-permute-start.2 = (bf16[768,1536]{1,0:T(8,128)(2,1)}, bf16[768,1536]{1,0:T(8,128)(2,1)S(1)}, u32[]{:S(2)}, u32[]{:S(2)}) collective-permute-start(bf16[768,1536]{1,0:T(8,128)(2,1)} %get-tuple-element.33), channel_id=1, source_target_pairs={{0,192},{64,0},{128,64},{192,128},{1,193},{65,1},{129,65},{193,129... | collective-permute-start | bytes 7077896 | tf_op jit(solution)/shard_map/ppermute | solution.py:227
  65.6 53.5 %copy-start.6 = (bf16[768,1536]{1,0:T(8,128)(2,1)}, bf16[768,1536]{1,0:T(8,128)(2,1)S(1)}, u32[]{:S(2)}) copy-start(bf16[768,1536]{1,0:T(8,128)(2,1)S(1)} %collective-permute-done.refs_1_) | copy-start | bytes 7077892
  124.5 9.4 %all-to-all-start = ((bf16[4,18,128]{2,1,0:T(8,128)(2,1)}), bf16[4,18,128]{2,1,0:T(8,128)(2,1)S(1)}, u32[]{:S(2)}, u32[]{:S(2)}) async-start(bf16[4,18,128]{2,1,0:T(8,128)(2,1)} %pad_maximum_fusion.6), calls=%async_computation | async-start | bytes 49152 | tf_op jit(solution)/shard_map/all_to_all | solution.py:239
  137.2 53.8 %all-to-all-start.1 = ((bf16[64,96,128]{2,1,0:T(8,128)(2,1)}), bf16[64,96,128]{2,1,0:T(8,128)(2,1)}, u32[]{:S(2)}, u32[]{:S(2)}) async-start(bf16[64,96,128]{2,1,0:T(8,128)(2,1)} %bitcast.121), calls=%async_computation.1 | async-start | bytes 3145728 | tf_op jit(solution)/shard_map/all_to_all | solution.py:282
  151.3 173.5 %all-gather.11.cloned.1.call-start = ((), (), s32[]{:S(2)}) async-start(), calls=%async_computation.10 | async-start | bytes 11796480 | tf_op jit(solution)/shard_map/all_gather | solution.py:306
  196.3 225.9 %all-gather.13.cloned.1.call-start = ((), (), s32[]{:S(2)}) async-start(), calls=%async_computation.11 | async-start | bytes 11796480 | tf_op jit(solution)/shard_map/all_gather | solution.py:306
  230.6 10.8 %copy-start.17 = (bf16[1,2048,64]{1,2,0:T(8,128)(2,1)S(1)}, bf16[1,2048,64]{1,2,0:T(8,128)(2,1)}, u32[]{:S(2)}) copy-start(bf16[1,2048,64]{1,2,0:T(8,128)(2,1)} %param.10) | copy-start | bytes 786436
  230.6 50.6 %all-to-all-start.2 = ((bf16[64,96,128]{2,1,0:T(8,128)(2,1)}), bf16[64,96,128]{2,1,0:T(8,128)(2,1)S(1)}, u32[]{:S(2)}, u32[]{:S(2)}) async-start(bf16[64,96,128]{2,1,0:T(8,128)(2,1)} %bitcast.15), calls=%async_computation.2 | async-start | bytes 3145728 | tf_op jit(solution)/shard_map/all_to_all | solution.py:282
  241.8 9.4 %collective-permute-start.3 = (bf16[512,128]{1,0:T(8,128)(2,1)S(1)}, bf16[512,128]{1,0:T(8,128)(2,1)S(1)}, u32[]{:S(2)}, u32[]{:S(2)}) collective-permute-start(bf16[512,128]{1,0:T(8,128)(2,1)S(1)} %reshape.144), channel_id=1, source_target_pairs={{0,64},{64,128},{128,192},{192,0},{1,65},{65,129},{129,193},{193,1... | collective-permute-start | bytes 393224 | tf_op jit(solution)/shard_map/ppermute | solution.py:227
  243.1 13.6 %collective-permute-start.4 = (bf16[512,128]{1,0:T(8,128)(2,1)S(1)}, bf16[512,128]{1,0:T(8,128)(2,1)S(1)}, u32[]{:S(2)}, u32[]{:S(2)}) collective-permute-start(bf16[512,128]{1,0:T(8,128)(2,1)S(1)} %reshape.144), channel_id=1, source_target_pairs={{0,128},{64,192},{128,0},{192,64},{1,129},{65,193},{129,1},{193,65... | collective-permute-start | bytes 393224 | tf_op jit(solution)/shard_map/ppermute | solution.py:227
  244.8 12.8 %collective-permute-start.5 = (bf16[512,128]{1,0:T(8,128)(2,1)S(1)}, bf16[512,128]{1,0:T(8,128)(2,1)S(1)}, u32[]{:S(2)}, u32[]{:S(2)}) collective-permute-start(bf16[512,128]{1,0:T(8,128)(2,1)S(1)} %reshape.144), channel_id=1, source_target_pairs={{0,192},{64,0},{128,64},{192,128},{1,193},{65,1},{129,65},{193,129... | collective-permute-start | bytes 393224 | tf_op jit(solution)/shard_map/ppermute | solution.py:227
  258.5 3.4 collective-permute-start.6
  283.6 45.9 %all-to-all-start.3 = ((bf16[64,96,128]{2,1,0:T(8,128)(2,1)}), bf16[64,96,128]{2,1,0:T(8,128)(2,1)S(1)}, u32[]{:S(2)}, u32[]{:S(2)}) async-start(bf16[64,96,128]{2,1,0:T(8,128)(2,1)} %bitcast.123), calls=%async_computation.3 | async-start | bytes 3145728 | tf_op jit(solution)/shard_map/all_to_all | solution.py:282
  289.7 235.3 %all-gather.15.cloned.1.call-start = ((), (), s32[]{:S(2)}) async-start(), calls=%async_computation.12 | async-start | bytes 11796480 | tf_op jit(solution)/shard_map/all_gather | solution.py:306
  336.9 46.1 %all-to-all-start.4 = ((bf16[64,96,128]{2,1,0:T(8,128)(2,1)}), bf16[64,96,128]{2,1,0:T(8,128)(2,1)S(1)}, u32[]{:S(2)}, u32[]{:S(2)}) async-start(bf16[64,96,128]{2,1,0:T(8,128)(2,1)} %bitcast.27), calls=%async_computation.4 | async-start | bytes 3145728 | tf_op jit(solution)/shard_map/all_to_all | solution.py:282
  385.3 55.8 %all-to-all-start.5 = ((bf16[64,96,128]{2,1,0:T(8,128)(2,1)}), bf16[64,96,128]{2,1,0:T(8,128)(2,1)S(1)}, u32[]{:S(2)}, u32[]{:S(2)}) async-start(bf16[64,96,128]{2,1,0:T(8,128)(2,1)} %bitcast.124), calls=%async_computation.5 | async-start | bytes 3145728 | tf_op jit(solution)/shard_map/all_to_all | solution.py:282
  448.6 6.6 %copy-start.10 = (bf16[1,1024,128]{2,1,0:T(8,128)(2,1)S(1)}, bf16[1,1024,128]{2,1,0:T(8,128)(2,1)}, u32[]{:S(2)}) copy-start(bf16[1,1024,128]{2,1,0:T(8,128)(2,1)} %get-tuple-element.67) | copy-start | bytes 786436
  448.6 46.2 %all-to-all-start.6 = ((bf16[64,96,128]{2,1,0:T(8,128)(2,1)}), bf16[64,96,128]{2,1,0:T(8,128)(2,1)S(1)}, u32[]{:S(2)}, u32[]{:S(2)}) async-start(bf16[64,96,128]{2,1,0:T(8,128)(2,1)} %bitcast.35), calls=%async_computation.6 | async-start | bytes 3145728 | tf_op jit(solution)/shard_map/all_to_all | solution.py:282
  497.2 45.9 %all-to-all-start.7 = ((bf16[64,96,128]{2,1,0:T(8,128)(2,1)}), bf16[64,96,128]{2,1,0:T(8,128)(2,1)S(1)}, u32[]{:S(2)}, u32[]{:S(2)}) async-start(bf16[64,96,128]{2,1,0:T(8,128)(2,1)} %bitcast.122), calls=%async_computation.7 | async-start | bytes 3145728 | tf_op jit(solution)/shard_map/all_to_all | solution.py:282
  504.1 46.5 %collective-permute-start.7 = (bf16[32,2048]{1,0:T(8,128)(2,1)}, bf16[32,2048]{1,0:T(8,128)(2,1)S(1)}, u32[]{:S(2)}, u32[]{:S(2)}) collective-permute-start(bf16[32,2048]{1,0:T(8,128)(2,1)} %get-tuple-element.79), channel_id=1, source_target_pairs={{0,64},{64,128},{128,192},{192,0},{1,65},{65,129},{129,193},{193,1... | collective-permute-start | bytes 393224 | tf_op jit(solution)/shard_map/ppermute | solution.py:227
  505.3 45.3 %collective-permute-start.8 = (bf16[32,2048]{1,0:T(8,128)(2,1)}, bf16[32,2048]{1,0:T(8,128)(2,1)S(1)}, u32[]{:S(2)}, u32[]{:S(2)}) collective-permute-start(bf16[32,2048]{1,0:T(8,128)(2,1)} %get-tuple-element.78), channel_id=1, source_target_pairs={{0,128},{64,192},{128,0},{192,64},{1,129},{65,193},{129,1},{193,65... | collective-permute-start | bytes 393224 | tf_op jit(solution)/shard_map/ppermute | solution.py:227
  506.7 43.9 %collective-permute-start.9 = (bf16[32,2048]{1,0:T(8,128)(2,1)S(1)}, bf16[32,2048]{1,0:T(8,128)(2,1)S(1)}, u32[]{:S(2)}, u32[]{:S(2)}) collective-permute-start(bf16[32,2048]{1,0:T(8,128)(2,1)S(1)} %get-tuple-element.77), channel_id=1, source_target_pairs={{0,192},{64,0},{128,64},{192,128},{1,193},{65,1},{129,65},{193,129... | collective-permute-start | bytes 393224 | tf_op jit(solution)/shard_map/ppermute | solution.py:227
  550.6 46.1 %all-to-all-start.8 = ((bf16[64,96,128]{2,1,0:T(8,128)(2,1)}), bf16[64,96,128]{2,1,0:T(8,128)(2,1)S(1)}, u32[]{:S(2)}, u32[]{:S(2)}) async-start(bf16[64,96,128]{2,1,0:T(8,128)(2,1)} %bitcast.43), calls=%async_computation.8 | async-start | bytes 3145728 | tf_op jit(solution)/shard_map/all_to_all | solution.py:282
  557.6 48.4 %copy-start.16 = (bf16[32,2048]{1,0:T(8,128)(2,1)S(1)}, bf16[32,2048]{1,0:T(8,128)(2,1)}, u32[]{:S(2)}) copy-start(bf16[32,2048]{1,0:T(8,128)(2,1)} %copy-done.15) | copy-start | bytes 393220
  596.6 10.3 %copy-start.1 = (bf16[4,32,2048]{2,1,0:T(8,128)(2,1)S(1)}, bf16[4,32,2048]{2,1,0:T(8,128)(2,1)}, u32[]{:S(2)}) copy-start(bf16[4,32,2048]{2,1,0:T(8,128)(2,1)} %param.7) | copy-start | bytes 1572868
  597.1 8.7 %collective-permute-start.10 = (bf16[32,2048]{1,0:T(8,128)(2,1)S(1)}, bf16[32,2048]{1,0:T(8,128)(2,1)S(1)}, u32[]{:S(2)}, u32[]{:S(2)}) collective-permute-start(bf16[32,2048]{1,0:T(8,128)(2,1)S(1)} %shard_map.83), channel_id=1, source_target_pairs={{0,192},{1,193},{2,194},{3,195},{4,196},{5,197},{6,198},{7,199},{8... | collective-permute-start | bytes 393224 | tf_op jit(solution)/shard_map/ppermute | solution.py:333
  600.5 5.4 collective-permute-start.11
  601.2 4.8 collective-permute-start.12
  (14 other events, 48.3 us)
Sparse Core Ops, SparseCore 0:
  123.0 98.7 all-gather.8
  223.6 101.1 all-gather.10
  326.6 95.5 all-gather.12
  423.8 101.1 all-gather.14

commit v4 on v3

--- a/solution.py
+++ b/solution.py
@@ -305,12 +305,6 @@
                 part = own_part(later, held)
                 gathered.append(lax.all_gather(part, "section", axis=0))
         expert_out = expert_mlp(arrived, [gathered[layer]])
-        if layer + 1 == sections:
-            moved = []
-            for by in range(1, sections):
-                pick = jnp.minimum(lax.rem(section + by, sections), sections - 2)
-                moved.append(shifted(lax.select_n(pick, *outs), by))
-            expert_out, moved = lax.optimization_barrier((expert_out, moved))
         returned = across(expert_out)
         if layer + 1 < sections:
             state, normed, sent = pl.pallas_call(
@@ -323,17 +317,8 @@
                 last_kernel, out_shape=tok_shape, compiler_params=params
             )(returned, mix_pair, state)
         outs.append(state)
-    last = sections - 1
-    mine = lax.select_n(section, *outs)
-    states = []
-    for micro in range(micro_count):
-        apart = lax.rem(section + sections - micro, sections)
-        home = lax.select_n(apart, mine, *moved)
-        if micro != last:
-            final = lax.ppermute(outs[last], "section", [(micro, last)])
-            home = jnp.where(section == last, final, home)
-        states.append(home)
-    return jnp.stack(states)[None]
+    states = lax.all_to_all(jnp.stack(outs), "section", 0, 0, tiled=True)
+    return states[None]
 
 
 def solution(mesh):

time: 620 us -> 610 us (0.984)
  starting transfers between devices: 98.8 us -> 79.1 us
  blocking collectives: 0 us -> 12.7 us
    all_gather x3, waiting for transfers between devices: 71.6 us -> 90.1 us  [on_device(): gathered.append(lax.all_gather(part, 'section', axis=0))]
    all_to_all x8, waiting for transfers between devices: 214 us -> 201 us  [across(): moved = lax.all_to_all(blocks, 'dp', 0, 0, tiled=True)]
    all_to_all x0 -> x1, blocking collectives: none -> 12.7 us  [on_device(): states = lax.all_to_all(jnp.stack(outs), 'section', 0, 0, tiled=True)]
    all_to_all x8, starting transfers between devices: 72.2 us -> 62 us  [across(): moved = lax.all_to_all(blocks, 'dp', 0, 0, tiled=True)]
    ppermute x9 -> x6, starting transfers between devices: 15.2 us -> 10.4 us  [shifted(): lax.ppermute(part, 'section', [(i, (i + by) % sections) for i in range(se...]
    ppermute x9 -> x6, waiting for transfers between devices: 111 us -> 111 us  [shifted(): lax.ppermute(part, 'section', [(i, (i + by) % sections) for i in range(se...]
  transfers between devices with their start and end apart: 26 -> 20, of which waited for: 20 -> 19; matrix products, arithmetic and copies ran while one was open for 3% -> 3% of each run, Pallas kernels for 6% -> 4%
where the time goes in v4:
time: 610 us; the launch traced here: 608 us
  waiting for transfers between devices  433 us (71%)
  starting transfers between devices  79.1 us (13%)
  Pallas kernels  41.8 us (7%)
  local copies, waits for them, and re-layouts  16.9 us (3%)
  between operations  13.8 us (2%)
  blocking collectives  12.7 us (2%)
  other arithmetic  10.1 us (2%)
    all_to_all x8, waiting for transfers between devices, across(): moved = lax.all_to_all(blocks, 'dp', 0, 0, tiled=True)  201 us
    ppermute x6, waiting for transfers between devices, shifted(): lax.ppermute(part, 'section', [(i, (i + by) % sections) for i in range(se...  111 us
    all_gather x3, waiting for transfers between devices, on_device(): gathered.append(lax.all_gather(part, 'section', axis=0))  90.1 us
    all_to_all x8, starting transfers between devices, across(): moved = lax.all_to_all(blocks, 'dp', 0, 0, tiled=True)  62 us
    pallas_call x4, Pallas kernels, expert_mlp(): pl.pallas_call(lambda *refs: mlp_kernel(split, *refs), out_shape=jax.Shap...  28.9 us
    all_gather x1, waiting for transfers between devices, on_device(): gathered = [lax.all_gather(first_part, 'section', axis=0)]  24.8 us
    all_to_all x1, blocking collectives, on_device(): states = lax.all_to_all(jnp.stack(outs), 'section', 0, 0, tiled=True)  12.7 us
  transfers between devices with their start and end apart: 20, of which 19 were waited for; matrix products, arithmetic and copies ran while one was open for 3% of the time, Pallas kernels for 4%

profile of v4, /device:TPU:1, one launch (start us, length us, event | category | flops | bytes accessed | tf_op | source)
XLA Modules:
  0.0 608.4 jit_solution(17202135020096269617)
XLA Ops:
  6.5 6.6 %shard_map.73 = (bf16[768,1536]{1,0:T(8,128)(2,1)S(1)}, bf16[768,1536]{1,0:T(8,128)(2,1)S(1)}, bf16[768,1536]{1,0:T(8,128)(2,1)}, bf16[768,1536]{1,0:T(8,128)(2,1)}) custom-call(s32[1]{0:T(128)} %bitcast.1.first_ref.which_ref, bf16[2048,768]{1,0:T(8,128)(2,1)} %bitcast.136, bf16[2048,768]{1,0:T(8,128)(2,1)} %bitcast.137, bf16[768,2048]{1,0:T(8,128)(2,1)} %bitcast.138), custom_call_target="tpu_custom_call" | custom-call | tf_op jit(solution)/shard_map/pallas_call | solution.py:170
  18.9 46.7 %collective-permute-done.refs_1_ = bf16[768,1536]{1,0:T(8,128)(2,1)S(1)} collective-permute-done((bf16[768,1536]{1,0:T(8,128)(2,1)S(1)}, bf16[768,1536]{1,0:T(8,128)(2,1)S(1)}, u32[]{:S(2)}, u32[]{:S(2)}) %collective-permute-start) | collective-permute-done | bytes 2359328 | tf_op jit(solution)/shard_map/ppermute | solution.py:227
  65.6 53.5 %collective-permute-done.1.refs_2_ = bf16[768,1536]{1,0:T(8,128)(2,1)S(1)} collective-permute-done((bf16[768,1536]{1,0:T(8,128)(2,1)}, bf16[768,1536]{1,0:T(8,128)(2,1)S(1)}, u32[]{:S(2)}, u32[]{:S(2)}) %collective-permute-start.1) | collective-permute-done | bytes 2359328 | tf_op jit(solution)/shard_map/ppermute | solution.py:227
  124.5 5.1 all-to-all-start
  137.2 14.1 %all-to-all-start.1 = ((bf16[64,96,128]{2,1,0:T(8,128)(2,1)}), bf16[64,96,128]{2,1,0:T(8,128)(2,1)}, u32[]{:S(2)}, u32[]{:S(2)}) async-start(bf16[64,96,128]{2,1,0:T(8,128)(2,1)} %bitcast.119), calls=%async_computation.1 | async-start | bytes 3145728 | tf_op jit(solution)/shard_map/all_to_all | solution.py:282
  151.4 39.7 %all-to-all-done.1 = bf16[64,96,128]{2,1,0:T(8,128)(2,1)} async-done(((bf16[64,96,128]{2,1,0:T(8,128)(2,1)}), bf16[64,96,128]{2,1,0:T(8,128)(2,1)}, u32[]{:S(2)}, u32[]{:S(2)}) %all-to-all-start.1) | async-done | bytes 1572896 | tf_op jit(solution)/shard_map/all_to_all | solution.py:282
  191.0 5.2 select_select_fusion
  197.0 24.8 %all-gather.9.cloned.1.call-done = bf16[3072,1536]{1,0:T(8,128)(2,1)} async-done(((bf16[768,1536]{1,0:T(8,128)(2,1)}), bf16[3072,1536]{1,0:T(8,128)(2,1)}) %all-gather.9.cloned.1.call-update) | async-done | bytes 9437200 | tf_op jit(solution)/shard_map/all_gather | solution.py:251
  221.8 8.8 %shard_map.76 = bf16[384,16,128]{2,1,0:T(8,128)(2,1)} custom-call(bf16[384,16,128]{2,1,0:T(8,128)(2,1)} %bitcast.13.refs_0_, bf16[4,768,1536]{2,1,0:T(8,128)(2,1)} %bitcast.133), custom_call_target="tpu_custom_call" | custom-call | tf_op jit(solution)/shard_map/pallas_call | solution.py:119
  230.7 10.8 %all-to-all-start.2 = ((bf16[64,96,128]{2,1,0:T(8,128)(2,1)}), bf16[64,96,128]{2,1,0:T(8,128)(2,1)S(1)}, u32[]{:S(2)}, u32[]{:S(2)}) async-start(bf16[64,96,128]{2,1,0:T(8,128)(2,1)} %bitcast.15), calls=%async_computation.2 | async-start | bytes 3145728 | tf_op jit(solution)/shard_map/all_to_all | solution.py:282
  246.4 4.8 collective-permute-done.3
  251.2 5.5 collective-permute-done.4
  264.6 16.6 %all-to-all-done.2 = bf16[64,96,128]{2,1,0:T(8,128)(2,1)S(1)} async-done(((bf16[64,96,128]{2,1,0:T(8,128)(2,1)}), bf16[64,96,128]{2,1,0:T(8,128)(2,1)S(1)}, u32[]{:S(2)}, u32[]{:S(2)}) %all-to-all-start.2) | async-done | bytes 1572896 | tf_op jit(solution)/shard_map/all_to_all | solution.py:282
  283.6 6.1 %all-to-all-start.3 = ((bf16[64,96,128]{2,1,0:T(8,128)(2,1)}), bf16[64,96,128]{2,1,0:T(8,128)(2,1)S(1)}, u32[]{:S(2)}, u32[]{:S(2)}) async-start(bf16[64,96,128]{2,1,0:T(8,128)(2,1)} %bitcast.120), calls=%async_computation.3 | async-start | bytes 3145728 | tf_op jit(solution)/shard_map/all_to_all | solution.py:282
  290.3 34.5 %all-gather.11.cloned.1.call-done = bf16[3072,1536]{1,0:T(8,128)(2,1)} async-done(((bf16[768,1536]{1,0:T(8,128)(2,1)}), bf16[3072,1536]{1,0:T(8,128)(2,1)}) %all-gather.11.cloned.1.call-update) | async-done | bytes 9437200 | tf_op jit(solution)/shard_map/all_gather | solution.py:306
  324.8 4.7 all-to-all-done.3
  329.5 6.7 %shard_map.78 = bf16[384,16,128]{2,1,0:T(8,128)(2,1)S(1)} custom-call(bf16[384,16,128]{2,1,0:T(8,128)(2,1)S(1)} %bitcast.116, bf16[4,768,1536]{2,1,0:T(8,128)(2,1)} %bitcast.132), custom_call_target="tpu_custom_call" | custom-call | tf_op jit(solution)/shard_map/pallas_call | solution.py:119
  337.4 6.2 %all-to-all-start.4 = ((bf16[64,96,128]{2,1,0:T(8,128)(2,1)}), bf16[64,96,128]{2,1,0:T(8,128)(2,1)S(1)}, u32[]{:S(2)}, u32[]{:S(2)}) async-start(bf16[64,96,128]{2,1,0:T(8,128)(2,1)} %bitcast.114), calls=%async_computation.4 | async-start | bytes 3145728 | tf_op jit(solution)/shard_map/all_to_all | solution.py:282
  344.8 38.7 %all-to-all-done.4 = bf16[64,96,128]{2,1,0:T(8,128)(2,1)S(1)} async-done(((bf16[64,96,128]{2,1,0:T(8,128)(2,1)}), bf16[64,96,128]{2,1,0:T(8,128)(2,1)S(1)}, u32[]{:S(2)}, u32[]{:S(2)}) %all-to-all-start.4) | async-done | bytes 1572896 | tf_op jit(solution)/shard_map/all_to_all | solution.py:282
  385.8 6.1 %all-to-all-start.5 = ((bf16[64,96,128]{2,1,0:T(8,128)(2,1)}), bf16[64,96,128]{2,1,0:T(8,128)(2,1)S(1)}, u32[]{:S(2)}, u32[]{:S(2)}) async-start(bf16[64,96,128]{2,1,0:T(8,128)(2,1)} %bitcast.121), calls=%async_computation.5 | async-start | bytes 3145728 | tf_op jit(solution)/shard_map/all_to_all | solution.py:282
  391.9 30.3 %all-gather.13.cloned.1.call-done = bf16[3072,1536]{1,0:T(8,128)(2,1)} async-done(((bf16[768,1536]{1,0:T(8,128)(2,1)}), bf16[3072,1536]{1,0:T(8,128)(2,1)}) %all-gather.13.cloned.1.call-update) | async-done | bytes 9437200 | tf_op jit(solution)/shard_map/all_gather | solution.py:306
  422.2 9.5 %all-to-all-done.5 = bf16[64,96,128]{2,1,0:T(8,128)(2,1)S(1)} async-done(((bf16[64,96,128]{2,1,0:T(8,128)(2,1)}), bf16[64,96,128]{2,1,0:T(8,128)(2,1)S(1)}, u32[]{:S(2)}, u32[]{:S(2)}) %all-to-all-start.5) | async-done | bytes 1572896 | tf_op jit(solution)/shard_map/all_to_all | solution.py:282
  431.7 6.7 %shard_map.80 = bf16[384,16,128]{2,1,0:T(8,128)(2,1)S(1)} custom-call(bf16[384,16,128]{2,1,0:T(8,128)(2,1)S(1)} %bitcast.117, bf16[4,768,1536]{2,1,0:T(8,128)(2,1)} %bitcast.131), custom_call_target="tpu_custom_call" | custom-call | tf_op jit(solution)/shard_map/pallas_call | solution.py:119
  439.6 6.3 %all-to-all-start.6 = ((bf16[64,96,128]{2,1,0:T(8,128)(2,1)}), bf16[64,96,128]{2,1,0:T(8,128)(2,1)S(1)}, u32[]{:S(2)}, u32[]{:S(2)}) async-start(bf16[64,96,128]{2,1,0:T(8,128)(2,1)} %bitcast.115), calls=%async_computation.6 | async-start | bytes 3145728 | tf_op jit(solution)/shard_map/all_to_all | solution.py:282
  447.0 38.7 %all-to-all-done.6 = bf16[64,96,128]{2,1,0:T(8,128)(2,1)S(1)} async-done(((bf16[64,96,128]{2,1,0:T(8,128)(2,1)}), bf16[64,96,128]{2,1,0:T(8,128)(2,1)S(1)}, u32[]{:S(2)}, u32[]{:S(2)}) %all-to-all-start.6) | async-done | bytes 1572896 | tf_op jit(solution)/shard_map/all_to_all | solution.py:282
  488.0 6.1 %all-to-all-start.7 = ((bf16[64,96,128]{2,1,0:T(8,128)(2,1)}), bf16[64,96,128]{2,1,0:T(8,128)(2,1)S(1)}, u32[]{:S(2)}, u32[]{:S(2)}) async-start(bf16[64,96,128]{2,1,0:T(8,128)(2,1)} %bitcast.122), calls=%async_computation.7 | async-start | bytes 3145728 | tf_op jit(solution)/shard_map/all_to_all | solution.py:282
  494.1 25.3 %all-gather.15.cloned.1.call-done = bf16[3072,1536]{1,0:T(8,128)(2,1)} async-done(((bf16[768,1536]{1,0:T(8,128)(2,1)}), bf16[3072,1536]{1,0:T(8,128)(2,1)}) %all-gather.15.cloned.1.call-update) | async-done | bytes 9437200 | tf_op jit(solution)/shard_map/all_gather | solution.py:306
  519.4 14.5 %all-to-all-done.7 = bf16[64,96,128]{2,1,0:T(8,128)(2,1)S(1)} async-done(((bf16[64,96,128]{2,1,0:T(8,128)(2,1)}), bf16[64,96,128]{2,1,0:T(8,128)(2,1)S(1)}, u32[]{:S(2)}, u32[]{:S(2)}) %all-to-all-start.7) | async-done | bytes 1572896 | tf_op jit(solution)/shard_map/all_to_all | solution.py:282
  533.9 6.7 %shard_map.82 = bf16[384,16,128]{2,1,0:T(8,128)(2,1)S(1)} custom-call(bf16[384,16,128]{2,1,0:T(8,128)(2,1)S(1)} %bitcast.118, bf16[4,768,1536]{2,1,0:T(8,128)(2,1)} %bitcast.134), custom_call_target="tpu_custom_call" | custom-call | tf_op jit(solution)/shard_map/pallas_call | solution.py:119
  541.8 6.3 %all-to-all-start.8 = ((bf16[64,96,128]{2,1,0:T(8,128)(2,1)}), bf16[64,96,128]{2,1,0:T(8,128)(2,1)S(1)}, u32[]{:S(2)}, u32[]{:S(2)}) async-start(bf16[64,96,128]{2,1,0:T(8,128)(2,1)} %bitcast.113), calls=%async_computation.8 | async-start | bytes 3145728 | tf_op jit(solution)/shard_map/all_to_all | solution.py:282
  549.2 38.7 %all-to-all-done.8 = bf16[64,96,128]{2,1,0:T(8,128)(2,1)S(1)} async-done(((bf16[64,96,128]{2,1,0:T(8,128)(2,1)}), bf16[64,96,128]{2,1,0:T(8,128)(2,1)S(1)}, u32[]{:S(2)}, u32[]{:S(2)}) %all-to-all-start.8) | async-done | bytes 1572896 | tf_op jit(solution)/shard_map/all_to_all | solution.py:282
  588.5 12.7 %all_to_all.50 = bf16[4,32,2048]{2,1,0:T(8,128)(2,1)S(1)} all-to-all(bf16[4,32,2048]{2,1,0:T(8,128)(2,1)S(1)} %pad_maximum_fusion.1), channel_id=1, replica_groups=mesh['section'=4,'dp'=64] {'section'}, dimensions={0} | all-to-all | bytes 1048576 | tf_op jit(solution)/shard_map/all_to_all | solution.py:320
  (152 shorter events, 47.7 us)
Async XLA Ops:
  6.5 123.1 %copy-start = (bf16[4,32,2048]{2,1,0:T(8,128)(2,1)S(1)}, bf16[4,32,2048]{2,1,0:T(8,128)(2,1)}, u32[]{:S(2)}) copy-start(bf16[4,32,2048]{2,1,0:T(8,128)(2,1)} %param.7) | copy-start | bytes 1572868
  6.5 215.3 %all-gather.9.cloned.1.call-start = ((), (), s32[]{:S(2)}) async-start(), calls=%async_computation.10 | async-start | bytes 11796480 | tf_op jit(solution)/shard_map/all_gather | solution.py:251
  13.1 52.5 %collective-permute-start = (bf16[768,1536]{1,0:T(8,128)(2,1)S(1)}, bf16[768,1536]{1,0:T(8,128)(2,1)S(1)}, u32[]{:S(2)}, u32[]{:S(2)}) collective-permute-start(bf16[768,1536]{1,0:T(8,128)(2,1)S(1)} %get-tuple-element.27), channel_id=1, source_target_pairs={{0,64},{64,128},{128,192},{192,0},{1,65},{65,129},{129,193},{193,1... | collective-permute-start | bytes 7077896 | tf_op jit(solution)/shard_map/ppermute | solution.py:227
  15.3 103.8 %collective-permute-start.1 = (bf16[768,1536]{1,0:T(8,128)(2,1)}, bf16[768,1536]{1,0:T(8,128)(2,1)S(1)}, u32[]{:S(2)}, u32[]{:S(2)}) collective-permute-start(bf16[768,1536]{1,0:T(8,128)(2,1)} %get-tuple-element.28), channel_id=1, source_target_pairs={{0,128},{64,192},{128,0},{192,64},{1,129},{65,193},{129,1},{193,65... | collective-permute-start | bytes 7077896 | tf_op jit(solution)/shard_map/ppermute | solution.py:227
  17.9 101.2 %collective-permute-start.2 = (bf16[768,1536]{1,0:T(8,128)(2,1)}, bf16[768,1536]{1,0:T(8,128)(2,1)S(1)}, u32[]{:S(2)}, u32[]{:S(2)}) collective-permute-start(bf16[768,1536]{1,0:T(8,128)(2,1)} %get-tuple-element.29), channel_id=1, source_target_pairs={{0,192},{64,0},{128,64},{192,128},{1,193},{65,1},{129,65},{193,129... | collective-permute-start | bytes 7077896 | tf_op jit(solution)/shard_map/ppermute | solution.py:227
  65.6 53.5 %copy-start.9 = (bf16[768,1536]{1,0:T(8,128)(2,1)}, bf16[768,1536]{1,0:T(8,128)(2,1)S(1)}, u32[]{:S(2)}) copy-start(bf16[768,1536]{1,0:T(8,128)(2,1)S(1)} %collective-permute-done.refs_1_) | copy-start | bytes 7077892
  119.1 1.5 copy-start.10
  119.1 2.1 copy-start.11
  124.5 9.4 %all-to-all-start = ((bf16[4,18,128]{2,1,0:T(8,128)(2,1)}), bf16[4,18,128]{2,1,0:T(8,128)(2,1)S(1)}, u32[]{:S(2)}, u32[]{:S(2)}) async-start(bf16[4,18,128]{2,1,0:T(8,128)(2,1)} %pad_maximum_fusion.7), calls=%async_computation | async-start | bytes 49152 | tf_op jit(solution)/shard_map/all_to_all | solution.py:239
  137.2 53.8 %all-to-all-start.1 = ((bf16[64,96,128]{2,1,0:T(8,128)(2,1)}), bf16[64,96,128]{2,1,0:T(8,128)(2,1)}, u32[]{:S(2)}, u32[]{:S(2)}) async-start(bf16[64,96,128]{2,1,0:T(8,128)(2,1)} %bitcast.119), calls=%async_computation.1 | async-start | bytes 3145728 | tf_op jit(solution)/shard_map/all_to_all | solution.py:282
  151.3 173.5 %all-gather.11.cloned.1.call-start = ((), (), s32[]{:S(2)}) async-start(), calls=%async_computation.11 | async-start | bytes 11796480 | tf_op jit(solution)/shard_map/all_gather | solution.py:306
  196.3 225.9 %all-gather.13.cloned.1.call-start = ((), (), s32[]{:S(2)}) async-start(), calls=%async_computation.12 | async-start | bytes 11796480 | tf_op jit(solution)/shard_map/all_gather | solution.py:306
  230.7 10.8 %copy-start.18 = (bf16[1,2048,64]{1,2,0:T(8,128)(2,1)S(1)}, bf16[1,2048,64]{1,2,0:T(8,128)(2,1)}, u32[]{:S(2)}) copy-start(bf16[1,2048,64]{1,2,0:T(8,128)(2,1)} %param.10) | copy-start | bytes 786436
  230.7 50.6 %all-to-all-start.2 = ((bf16[64,96,128]{2,1,0:T(8,128)(2,1)}), bf16[64,96,128]{2,1,0:T(8,128)(2,1)S(1)}, u32[]{:S(2)}, u32[]{:S(2)}) async-start(bf16[64,96,128]{2,1,0:T(8,128)(2,1)} %bitcast.15), calls=%async_computation.2 | async-start | bytes 3145728 | tf_op jit(solution)/shard_map/all_to_all | solution.py:282
  241.8 9.4 %collective-permute-start.3 = (bf16[512,128]{1,0:T(8,128)(2,1)S(1)}, bf16[512,128]{1,0:T(8,128)(2,1)S(1)}, u32[]{:S(2)}, u32[]{:S(2)}) collective-permute-start(bf16[512,128]{1,0:T(8,128)(2,1)S(1)} %reshape.144), channel_id=1, source_target_pairs={{0,64},{64,128},{128,192},{192,0},{1,65},{65,129},{129,193},{193,1... | collective-permute-start | bytes 393224 | tf_op jit(solution)/shard_map/ppermute | solution.py:227
  243.1 13.6 %collective-permute-start.4 = (bf16[512,128]{1,0:T(8,128)(2,1)S(1)}, bf16[512,128]{1,0:T(8,128)(2,1)S(1)}, u32[]{:S(2)}, u32[]{:S(2)}) collective-permute-start(bf16[512,128]{1,0:T(8,128)(2,1)S(1)} %reshape.144), channel_id=1, source_target_pairs={{0,128},{64,192},{128,0},{192,64},{1,129},{65,193},{129,1},{193,65... | collective-permute-start | bytes 393224 | tf_op jit(solution)/shard_map/ppermute | solution.py:227
  244.6 12.7 %collective-permute-start.5 = (bf16[512,128]{1,0:T(8,128)(2,1)S(1)}, bf16[512,128]{1,0:T(8,128)(2,1)S(1)}, u32[]{:S(2)}, u32[]{:S(2)}) collective-permute-start(bf16[512,128]{1,0:T(8,128)(2,1)S(1)} %reshape.144), channel_id=1, source_target_pairs={{0,192},{64,0},{128,64},{192,128},{1,193},{65,1},{129,65},{193,129... | collective-permute-start | bytes 393224 | tf_op jit(solution)/shard_map/ppermute | solution.py:227
  258.3 3.4 collective-permute-start.6
  283.6 45.9 %all-to-all-start.3 = ((bf16[64,96,128]{2,1,0:T(8,128)(2,1)}), bf16[64,96,128]{2,1,0:T(8,128)(2,1)S(1)}, u32[]{:S(2)}, u32[]{:S(2)}) async-start(bf16[64,96,128]{2,1,0:T(8,128)(2,1)} %bitcast.120), calls=%async_computation.3 | async-start | bytes 3145728 | tf_op jit(solution)/shard_map/all_to_all | solution.py:282
  289.7 229.7 %all-gather.15.cloned.1.call-start = ((), (), s32[]{:S(2)}) async-start(), calls=%async_computation.13 | async-start | bytes 11796480 | tf_op jit(solution)/shard_map/all_gather | solution.py:306
  337.4 6.3 %copy-start.17 = (f32[1,32,64,6]{1,3,2,0:T(8,128)S(1)}, f32[1,32,64,6]{1,3,2,0:T(8,128)}, u32[]{:S(2)}) copy-start(f32[1,32,64,6]{1,3,2,0:T(8,128)} %get-tuple-element.52) | copy-start | bytes 147460
  337.4 6.4 %copy-start.14 = (bf16[1,1024,128]{2,1,0:T(8,128)(2,1)S(1)}, bf16[1,1024,128]{2,1,0:T(8,128)(2,1)}, u32[]{:S(2)}) copy-start(bf16[1,1024,128]{2,1,0:T(8,128)(2,1)} %get-tuple-element.56) | copy-start | bytes 786436
  337.4 46.1 %all-to-all-start.4 = ((bf16[64,96,128]{2,1,0:T(8,128)(2,1)}), bf16[64,96,128]{2,1,0:T(8,128)(2,1)S(1)}, u32[]{:S(2)}, u32[]{:S(2)}) async-start(bf16[64,96,128]{2,1,0:T(8,128)(2,1)} %bitcast.114), calls=%async_computation.4 | async-start | bytes 3145728 | tf_op jit(solution)/shard_map/all_to_all | solution.py:282
  385.8 45.9 %all-to-all-start.5 = ((bf16[64,96,128]{2,1,0:T(8,128)(2,1)}), bf16[64,96,128]{2,1,0:T(8,128)(2,1)S(1)}, u32[]{:S(2)}, u32[]{:S(2)}) async-start(bf16[64,96,128]{2,1,0:T(8,128)(2,1)} %bitcast.121), calls=%async_computation.5 | async-start | bytes 3145728 | tf_op jit(solution)/shard_map/all_to_all | solution.py:282
  439.6 6.3 %copy-start.16 = (f32[1,32,64,6]{1,3,2,0:T(8,128)S(1)}, f32[1,32,64,6]{1,3,2,0:T(8,128)}, u32[]{:S(2)}) copy-start(f32[1,32,64,6]{1,3,2,0:T(8,128)} %get-tuple-element.51) | copy-start | bytes 147460
  439.6 6.4 %copy-start.13 = (bf16[1,1024,128]{2,1,0:T(8,128)(2,1)S(1)}, bf16[1,1024,128]{2,1,0:T(8,128)(2,1)}, u32[]{:S(2)}) copy-start(bf16[1,1024,128]{2,1,0:T(8,128)(2,1)} %get-tuple-element.57) | copy-start | bytes 786436
  439.6 46.1 %all-to-all-start.6 = ((bf16[64,96,128]{2,1,0:T(8,128)(2,1)}), bf16[64,96,128]{2,1,0:T(8,128)(2,1)S(1)}, u32[]{:S(2)}, u32[]{:S(2)}) async-start(bf16[64,96,128]{2,1,0:T(8,128)(2,1)} %bitcast.115), calls=%async_computation.6 | async-start | bytes 3145728 | tf_op jit(solution)/shard_map/all_to_all | solution.py:282
  488.0 45.9 %all-to-all-start.7 = ((bf16[64,96,128]{2,1,0:T(8,128)(2,1)}), bf16[64,96,128]{2,1,0:T(8,128)(2,1)S(1)}, u32[]{:S(2)}, u32[]{:S(2)}) async-start(bf16[64,96,128]{2,1,0:T(8,128)(2,1)} %bitcast.122), calls=%async_computation.7 | async-start | bytes 3145728 | tf_op jit(solution)/shard_map/all_to_all | solution.py:282
  541.8 6.3 %copy-start.15 = (f32[1,32,64,6]{1,3,2,0:T(8,128)S(1)}, f32[1,32,64,6]{1,3,2,0:T(8,128)}, u32[]{:S(2)}) copy-start(f32[1,32,64,6]{1,3,2,0:T(8,128)} %get-tuple-element.50) | copy-start | bytes 147460
  541.8 6.4 %copy-start.12 = (bf16[1,1024,128]{2,1,0:T(8,128)(2,1)S(1)}, bf16[1,1024,128]{2,1,0:T(8,128)(2,1)}, u32[]{:S(2)}) copy-start(bf16[1,1024,128]{2,1,0:T(8,128)(2,1)} %get-tuple-element.54) | copy-start | bytes 786436
  541.8 46.1 %all-to-all-start.8 = ((bf16[64,96,128]{2,1,0:T(8,128)(2,1)}), bf16[64,96,128]{2,1,0:T(8,128)(2,1)S(1)}, u32[]{:S(2)}, u32[]{:S(2)}) async-start(bf16[64,96,128]{2,1,0:T(8,128)(2,1)} %bitcast.113), calls=%async_computation.8 | async-start | bytes 3145728 | tf_op jit(solution)/shard_map/all_to_all | solution.py:282
  587.9 14.1 %copy-start.1 = (bf16[4,32,2048]{2,1,0:T(8,128)(2,1)S(1)}, bf16[4,32,2048]{2,1,0:T(8,128)(2,1)}, u32[]{:S(2)}) copy-start(bf16[4,32,2048]{2,1,0:T(8,128)(2,1)} %param.7) | copy-start | bytes 1572868
  (9 other events, 10.0 us)
Sparse Core Ops, SparseCore 0:
  123.0 98.7 all-gather.8
  223.6 101.1 all-gather.10
  326.6 95.5 all-gather.12
  423.9 95.5 all-gather.14
